TPU v7x, 32 devices: a whole 2x2x4 slice. The times are simulated.
32 devices in a mesh: ctx: 8 (over y, x, core), fsdp: 4 (over z).
Axes of the slice: x: 2, y: 2, z: 4, core: 2. Of those that a mesh axis runs over, the one named last changes fastest.
Arguments:
- tokens: bfloat16 [4, 1024, 2048], P('fsdp', 'ctx'), may hold values from -6 to 6
- positions: int32 [4, 1024], P('fsdp', 'ctx'), may hold values from 0 to 1021, as said below
- routes: int32 [4, 1024, 4], P('fsdp', 'ctx'), may hold values from 0 to 7, all different within a row; in each aligned block of 128 rows (0 to 127, 128 to 255, ..., all dimensions but the last counted through in order) at most 128 rows name the same one
- cotangent: bfloat16 [4, 1024, 2048], P('fsdp', 'ctx'), may hold values from -6 to 6
- attn_gain: bfloat16 [2048], P(('ctx', 'fsdp')), may hold values from 0.5 to 1.5
- query_weight: bfloat16 [2048, 2048], P(('ctx', 'fsdp')), may hold values from -0.125 to 0.125
- key_weight: bfloat16 [2048, 2048], P(('ctx', 'fsdp')), may hold values from -0.125 to 0.125
- value_weight: bfloat16 [2048, 2048], P(('ctx', 'fsdp')), may hold values from -0.125 to 0.125
- query_bias: bfloat16 [2048], P(('ctx', 'fsdp')), may hold values from -3 to 3
- key_bias: bfloat16 [2048], P(('ctx', 'fsdp')), may hold values from -3 to 3
- value_bias: bfloat16 [2048], P(('ctx', 'fsdp')), may hold values from -3 to 3
- output_weight: bfloat16 [2048, 2048], P(('ctx', 'fsdp')), may hold values from -0.75 to 0.75
- ffn_gain: bfloat16 [2048], P(('ctx', 'fsdp')), may hold values from 0.5 to 1.5
- router_weight: bfloat16 [2048, 8], P(('ctx', 'fsdp')), may hold values from -0.0625 to 0.0625
- expert_gate: bfloat16 [8, 2048, 1408], P('ctx', 'fsdp'), may hold values from -0.125 to 0.125
- expert_up: bfloat16 [8, 2048, 1408], P('ctx', 'fsdp'), may hold values from -0.125 to 0.125
- expert_down: bfloat16 [8, 1408, 2048], P('ctx', 'fsdp'), may hold values from -0.5 to 0.5
- shared_gate: bfloat16 [2048, 5632], P(('ctx', 'fsdp')), may hold values from -0.125 to 0.125
- shared_up: bfloat16 [2048, 5632], P(('ctx', 'fsdp')), may hold values from -0.125 to 0.125
- shared_down: bfloat16 [5632, 2048], P(('ctx', 'fsdp')), may hold values from -0.15625 to 0.15625
- shared_sigmoid: bfloat16 [2048], P(('ctx', 'fsdp')), may hold values from -0.125 to 0.125
Outputs:
- layer_out: bfloat16 [4, 1024, 2048], P('fsdp', 'ctx')
- grad_tokens: float32 [4, 1024, 2048], P('fsdp', 'ctx')
- grad_attn_gain: float32 [2048], P(('ctx', 'fsdp'))
- grad_query_weight: float32 [2048, 2048], P(('ctx', 'fsdp'))
- grad_key_weight: float32 [2048, 2048], P(('ctx', 'fsdp'))
- grad_value_weight: float32 [2048, 2048], P(('ctx', 'fsdp'))
- grad_query_bias: float32 [2048], P(('ctx', 'fsdp'))
- grad_key_bias: float32 [2048], P(('ctx', 'fsdp'))
- grad_value_bias: float32 [2048], P(('ctx', 'fsdp'))
- grad_output_weight: float32 [2048, 2048], P(('ctx', 'fsdp'))
- grad_ffn_gain: float32 [2048], P(('ctx', 'fsdp'))
- grad_router_weight: float32 [2048, 8], P(('ctx', 'fsdp'))
- grad_expert_gate: float32 [8, 2048, 1408], P('ctx', 'fsdp')
- grad_expert_up: float32 [8, 2048, 1408], P('ctx', 'fsdp')
- grad_expert_down: float32 [8, 1408, 2048], P('ctx', 'fsdp')
- grad_shared_gate: float32 [2048, 5632], P(('ctx', 'fsdp'))
- grad_shared_up: float32 [2048, 5632], P(('ctx', 'fsdp'))
- grad_shared_down: float32 [5632, 2048], P(('ctx', 'fsdp'))
- grad_shared_sigmoid: float32 [2048], P(('ctx', 'fsdp'))
Inputs may be any that keep to these rules, and one draw needn't show every extreme that they name: Each row of 1024 positions is three documents in a row, counting 0, 1, 2, ... from each document's first token; the first ends within the first 128 places and the last begins within the last 128 places. In some row the first document is one token and the last is one token. `routes`: A token's 4 experts differ. In the rows of one device (128 tokens, aligned) no expert is named more than 128 times, a bound that some block reaches.
All inputs are finite; a program needn't handle non-finite values.
Results may differ from a plain program's by a relative error of at most 0.04.
Values may be sent and summed in bfloat16 or wider, within the bound.
A program may use at most 448 MiB of HBM per device.

v0:
```python
import math

import jax
import jax.numpy as jnp
from jax import lax
from jax.sharding import PartitionSpec as P

HEADS = 16
HEAD = 128


EPS = 1e-06
ROPE_BASE = 1000000.0
MASKED = -1e30


def from_behind(value, axis, steps):
    count = lax.axis_size(axis)
    leading, last = (max(0, -steps), min(count, count - steps))
    return lax.ppermute(value, axis, [(source, source + steps) for source in range(leading, last)])


def shifted(shard, axis, by):
    length = lax.axis_size(axis)
    return lax.ppermute(shard, axis, [(i, (i + by) % length) for i in range(length)])


def rms_scale(values):
    return lax.rsqrt(jnp.mean(values * values, axis=-1, keepdims=True) + EPS)


def rope_tables(places, head_size):
    half = head_size // 2
    freqs = jnp.exp(jnp.arange(half, dtype=jnp.float32) * (-2.0 * math.log(ROPE_BASE) / head_size))
    angles = places.astype(jnp.float32)[:, None] * freqs[None, :]
    return (jnp.cos(angles), jnp.sin(angles))


def rotate(values, cosine, sine):
    half = values.shape[-1] // 2
    first = values[..., :half]
    second = values[..., half:]
    cosine = cosine[:, None, :]
    sine = sine[:, None, :]
    return jnp.concatenate(
        [first * cosine - second * sine, second * cosine + first * sine], axis=-1
    )


def rotate_back(grads, cosine, sine):
    half = grads.shape[-1] // 2
    first = grads[..., :half]
    second = grads[..., half:]
    cosine = cosine[:, None, :]
    sine = sine[:, None, :]
    return jnp.concatenate(
        [first * cosine + second * sine, second * cosine - first * sine], axis=-1
    )


def silu_slope(values):
    sigma = jax.nn.sigmoid(values)
    return sigma * (1.0 + values * (1.0 - sigma))


def visible(query_glob, starts, key_glob):
    return (key_glob[None, :] <= query_glob[:, None]) & (key_glob[None, :] >= starts[:, None])


def head_scores(queries, keys):
    return jnp.einsum("qhd,khd->hqk", queries, keys, preferred_element_type=jnp.float32)


def times_back(left, right):
    return jnp.dot(left, right.T, preferred_element_type=jnp.float32)


def outer_sum(left, right):
    return jnp.dot(left.T, right, preferred_element_type=jnp.float32)


def to_owners(rows, cycle_size, local_experts, capacity, width):
    return (
        rows.reshape(local_experts, cycle_size, capacity, width)
        .transpose(1, 0, 2, 3)
        .reshape(cycle_size, local_experts * capacity, width)
    )


def from_senders(rows, cycle_size, local_experts, capacity, width):
    return (
        rows.reshape(cycle_size, local_experts, capacity, width)
        .transpose(1, 0, 2, 3)
        .reshape(local_experts, cycle_size * capacity, width)
    )


def body(
    tokens,
    positions,
    routes,
    cotangent,
    attn_gain,
    query_weight,
    key_weight,
    value_weight,
    query_bias,
    key_bias,
    value_bias,
    output_weight,
    ffn_gain,
    router_weight,
    expert_gate,
    expert_up,
    expert_down,
    shared_gate,
    shared_up,
    shared_down,
    shared_sigmoid,
):
    cycle_size = lax.axis_size("ctx")
    cycle_index = lax.axis_index("ctx")
    seq_rows = tokens.shape[1]
    width = tokens.shape[2]
    top = routes.shape[2]
    expert_count = router_weight.shape[1]
    local_experts = expert_gate.shape[0]
    capacity = max(2, 2 * seq_rows * top // expert_count)
    slot_total = expert_count * capacity
    scale = 1.0 / math.sqrt(HEAD)
    states = tokens[0].astype(jnp.float32)
    places = positions[0]
    chosen = routes[0]
    grad_out = cotangent[0].astype(jnp.float32)
    gain_in, w_query, w_key, w_value, b_query, b_key, b_value, w_output = (
        lax.all_gather(attn_gain, ("ctx", "fsdp"), axis=0, tiled=True),
        lax.all_gather(query_weight, ("ctx", "fsdp"), axis=0, tiled=True),
        lax.all_gather(key_weight, ("ctx", "fsdp"), axis=0, tiled=True),
        lax.all_gather(value_weight, ("ctx", "fsdp"), axis=0, tiled=True),
        lax.all_gather(query_bias, ("ctx", "fsdp"), axis=0, tiled=True),
        lax.all_gather(key_bias, ("ctx", "fsdp"), axis=0, tiled=True),
        lax.all_gather(value_bias, ("ctx", "fsdp"), axis=0, tiled=True),
        lax.all_gather(output_weight, ("ctx", "fsdp"), axis=0, tiled=True),
    )
    scale_in = rms_scale(states)
    unit_in = states * scale_in
    normed = (unit_in * gain_in.astype(jnp.float32)).astype(jnp.bfloat16)
    cosine, sine = rope_tables(places, HEAD)
    query_pre = jnp.dot(normed, w_query, preferred_element_type=jnp.float32) + b_query.astype(
        jnp.float32
    )
    key_pre = jnp.dot(normed, w_key, preferred_element_type=jnp.float32) + b_key.astype(jnp.float32)
    value_pre = jnp.dot(normed, w_value, preferred_element_type=jnp.float32) + b_value.astype(
        jnp.float32
    )
    queries = rotate(query_pre.reshape(seq_rows, HEADS, HEAD), cosine, sine).astype(jnp.bfloat16)
    keys = rotate(key_pre.reshape(seq_rows, HEADS, HEAD), cosine, sine).astype(jnp.bfloat16)
    values = value_pre.reshape(seq_rows, HEADS, HEAD).astype(jnp.bfloat16)
    offsets = jnp.arange(seq_rows, dtype=jnp.int32)
    query_glob = cycle_index * seq_rows + offsets
    starts = query_glob - places

    def attend(state, key_block, value_block, source):
        best, total, accum = state
        mask = visible(query_glob, starts, source * seq_rows + offsets)[None]
        scores = jnp.where(mask, head_scores(queries, key_block) * scale, MASKED)
        new_best = jnp.maximum(best, jnp.max(scores, axis=-1))
        weights = jnp.where(mask, jnp.exp(scores - new_best[..., None]), 0.0)
        shrink = jnp.exp(best - new_best)
        total = total * shrink + jnp.sum(weights, axis=-1)
        accum = accum * shrink.T[..., None] + jnp.einsum(
            "hqk,khd->qhd",
            weights.astype(jnp.bfloat16),
            value_block,
            preferred_element_type=jnp.float32,
        )
        return (new_best, total, accum)

    start_state = (
        jnp.full((HEADS, seq_rows), MASKED, jnp.float32),
        jnp.zeros((HEADS, seq_rows), jnp.float32),
        jnp.zeros((seq_rows, HEADS, HEAD), jnp.float32),
    )
    first_state = attend(start_state, keys, values, cycle_index)

    def cycle_step(step, carry):
        state, key_block, value_block = carry
        key_block, value_block = from_behind((key_block, value_block), "ctx", 1)
        source = (cycle_index - step) % cycle_size
        return (attend(state, key_block, value_block, source), key_block, value_block)

    final_state, key_left, value_left = lax.fori_loop(
        1, cycle_size, cycle_step, (first_state, keys, values)
    )
    best, total, accum = final_state
    attn_rows = accum / total.T[..., None]
    log_total = best + jnp.log(total)
    attn_low = attn_rows.reshape(seq_rows, width).astype(jnp.bfloat16)
    mid = states + jnp.dot(attn_low, w_output, preferred_element_type=jnp.float32)
    gain_mid, w_router, w_shared_gate, w_shared_up, w_shared_down, w_switch = (
        lax.all_gather(ffn_gain, ("ctx", "fsdp"), axis=0, tiled=True),
        lax.all_gather(router_weight, ("ctx", "fsdp"), axis=0, tiled=True),
        lax.all_gather(shared_gate, ("ctx", "fsdp"), axis=0, tiled=True),
        lax.all_gather(shared_up, ("ctx", "fsdp"), axis=0, tiled=True),
        lax.all_gather(shared_down, ("ctx", "fsdp"), axis=0, tiled=True),
        lax.all_gather(shared_sigmoid, ("ctx", "fsdp"), axis=0, tiled=True),
    )
    scale_mid = rms_scale(mid)
    unit_mid = mid * scale_mid
    normed2 = (unit_mid * gain_mid.astype(jnp.float32)).astype(jnp.bfloat16)
    logits = jnp.dot(normed2, w_router, preferred_element_type=jnp.float32)
    router_probs = jax.nn.softmax(logits, axis=-1)
    picks = chosen[:, :, None] == jnp.arange(expert_count, dtype=jnp.int32)[None, None, :]
    gates = jnp.sum(jnp.where(picks, router_probs[:, None, :], 0.0), axis=-1)
    flat_picks = picks.reshape(seq_rows * top, expert_count).astype(jnp.int32)
    ranks = jnp.cumsum(flat_picks, axis=0) - 1
    rank_of = jnp.sum(jnp.where(flat_picks > 0, ranks, 0), axis=-1)
    slot_of = chosen.reshape(-1) * capacity + rank_of
    select = (
        (slot_of[:, None] == jnp.arange(slot_total, dtype=jnp.int32)[None, :])
        .astype(jnp.bfloat16)
        .reshape(seq_rows, top, slot_total)
    )
    outgoing = jnp.einsum("tks,td->sd", select, normed2, preferred_element_type=jnp.float32).astype(
        jnp.bfloat16
    )
    incoming = lax.all_to_all(
        outgoing.reshape(cycle_size, slot_total // cycle_size, width),
        "ctx",
        split_axis=0,
        concat_axis=0,
        tiled=True,
    )
    gate_full, up_full, down_full = (
        lax.all_gather(expert_gate, "fsdp", axis=1, tiled=True),
        lax.all_gather(expert_up, "fsdp", axis=1, tiled=True),
        lax.all_gather(expert_down, "fsdp", axis=1, tiled=True),
    )
    expert_rows = from_senders(incoming, cycle_size, local_experts, capacity, width)
    gate_pre = jnp.einsum(
        "erd,edf->erf", expert_rows, gate_full, preferred_element_type=jnp.float32
    )
    up_pre = jnp.einsum("erd,edf->erf", expert_rows, up_full, preferred_element_type=jnp.float32)
    gate_act = jax.nn.silu(gate_pre)
    hidden = (gate_act * up_pre).astype(jnp.bfloat16)
    expert_out = jnp.einsum(
        "erf,efd->erd", hidden, down_full, preferred_element_type=jnp.float32
    ).astype(jnp.bfloat16)
    returned = lax.all_to_all(
        to_owners(expert_out, cycle_size, local_experts, capacity, width),
        "ctx",
        split_axis=0,
        concat_axis=0,
        tiled=True,
    )
    picked = jnp.einsum(
        "tks,sd->tkd",
        select,
        returned.reshape(slot_total, width),
        preferred_element_type=jnp.float32,
    )
    mixture = jnp.sum(gates[..., None] * picked, axis=1)
    shared_gate_pre = jnp.dot(normed2, w_shared_gate, preferred_element_type=jnp.float32)
    shared_up_pre = jnp.dot(normed2, w_shared_up, preferred_element_type=jnp.float32)
    shared_act = jax.nn.silu(shared_gate_pre)
    shared_hidden = (shared_act * shared_up_pre).astype(jnp.bfloat16)
    shared_out = jnp.dot(shared_hidden, w_shared_down, preferred_element_type=jnp.float32)
    switch = jax.nn.sigmoid(jnp.dot(normed2, w_switch, preferred_element_type=jnp.float32))
    result = mid + mixture + switch[:, None] * shared_out
    grad_gate = jnp.sum(grad_out[:, None, :] * picked, axis=-1)
    grad_slot = (gates[..., None] * grad_out[:, None, :]).astype(jnp.bfloat16)
    grad_sent = jnp.einsum(
        "tks,tkd->sd", select, grad_slot, preferred_element_type=jnp.float32
    ).astype(jnp.bfloat16)
    grad_arrived = lax.all_to_all(
        grad_sent.reshape(cycle_size, slot_total // cycle_size, width),
        "ctx",
        split_axis=0,
        concat_axis=0,
        tiled=True,
    )
    grad_expert = from_senders(grad_arrived, cycle_size, local_experts, capacity, width)
    grad_hidden = jnp.einsum(
        "erd,efd->erf", grad_expert, down_full, preferred_element_type=jnp.float32
    )
    grad_down_term = jnp.einsum(
        "erf,erd->efd", hidden, grad_expert, preferred_element_type=jnp.float32
    )
    grad_gate_pre = (grad_hidden * up_pre * silu_slope(gate_pre)).astype(jnp.bfloat16)
    grad_up_pre = (grad_hidden * gate_act).astype(jnp.bfloat16)
    grad_gate_term = jnp.einsum(
        "erd,erf->edf", expert_rows, grad_gate_pre, preferred_element_type=jnp.float32
    )
    grad_up_term = jnp.einsum(
        "erd,erf->edf", expert_rows, grad_up_pre, preferred_element_type=jnp.float32
    )
    grad_rows = (
        jnp.einsum("erf,edf->erd", grad_gate_pre, gate_full, preferred_element_type=jnp.float32)
        + jnp.einsum("erf,edf->erd", grad_up_pre, up_full, preferred_element_type=jnp.float32)
    ).astype(jnp.bfloat16)
    grad_back = lax.all_to_all(
        to_owners(grad_rows, cycle_size, local_experts, capacity, width),
        "ctx",
        split_axis=0,
        concat_axis=0,
        tiled=True,
    )
    grad_moe = jnp.einsum(
        "tks,sd->td",
        select,
        grad_back.reshape(slot_total, width),
        preferred_element_type=jnp.float32,
    )
    grad_expert_gate, grad_expert_up, grad_expert_down = (
        lax.psum_scatter(
            grad_gate_term.astype(jnp.bfloat16), "fsdp", scatter_dimension=1, tiled=True
        ).astype(jnp.float32),
        lax.psum_scatter(
            grad_up_term.astype(jnp.bfloat16), "fsdp", scatter_dimension=1, tiled=True
        ).astype(jnp.float32),
        lax.psum_scatter(
            grad_down_term.astype(jnp.bfloat16), "fsdp", scatter_dimension=1, tiled=True
        ).astype(jnp.float32),
    )
    grad_probs = jnp.sum(jnp.where(picks, grad_gate[..., None], 0.0), axis=1)
    grad_logits = (
        router_probs * (grad_probs - jnp.sum(router_probs * grad_probs, axis=-1, keepdims=True))
    ).astype(jnp.bfloat16)
    grad_shared_out = (grad_out * switch[:, None]).astype(jnp.bfloat16)
    grad_switch = jnp.sum(grad_out * shared_out, axis=-1) * switch * (1.0 - switch)
    grad_shared_hidden = times_back(grad_shared_out, w_shared_down)
    grad_shared_gate_pre = (
        grad_shared_hidden * shared_up_pre * silu_slope(shared_gate_pre)
    ).astype(jnp.bfloat16)
    grad_shared_up_pre = (grad_shared_hidden * shared_act).astype(jnp.bfloat16)
    grad_shared_part = times_back(grad_shared_gate_pre, w_shared_gate) + times_back(
        grad_shared_up_pre, w_shared_up
    )
    term_shared_gate = outer_sum(normed2, grad_shared_gate_pre)
    term_shared_up = outer_sum(normed2, grad_shared_up_pre)
    term_shared_down = outer_sum(shared_hidden, grad_shared_out)
    grad_normed2 = (
        grad_moe
        + times_back(grad_logits, w_router)
        + grad_shared_part
        + grad_switch[:, None] * w_switch.astype(jnp.float32)[None, :]
    )
    term_router = outer_sum(normed2, grad_logits)
    term_switch = jnp.einsum("t,td->d", grad_switch, normed2.astype(jnp.float32))
    term_gain_mid = jnp.sum(grad_normed2 * unit_mid, axis=0)
    scaled_mid = grad_normed2 * gain_mid.astype(jnp.float32)
    grad_mid = grad_out + scale_mid * (
        scaled_mid - unit_mid * jnp.mean(scaled_mid * unit_mid, axis=-1, keepdims=True)
    )
    (
        grad_ffn_gain,
        grad_router_weight,
        grad_shared_gate,
        grad_shared_up,
        grad_shared_down,
        grad_shared_sigmoid,
    ) = (
        lax.psum_scatter(term_gain_mid, ("ctx", "fsdp"), scatter_dimension=0, tiled=True),
        lax.psum_scatter(term_router, ("ctx", "fsdp"), scatter_dimension=0, tiled=True),
        lax.psum_scatter(term_shared_gate, ("ctx", "fsdp"), scatter_dimension=0, tiled=True),
        lax.psum_scatter(term_shared_up, ("ctx", "fsdp"), scatter_dimension=0, tiled=True),
        lax.psum_scatter(term_shared_down, ("ctx", "fsdp"), scatter_dimension=0, tiled=True),
        lax.psum_scatter(term_switch, ("ctx", "fsdp"), scatter_dimension=0, tiled=True),
    )
    gain_in, w_query, w_key, w_value, b_query, b_key, b_value, w_output = (
        lax.all_gather(attn_gain, ("ctx", "fsdp"), axis=0, tiled=True),
        lax.all_gather(query_weight, ("ctx", "fsdp"), axis=0, tiled=True),
        lax.all_gather(key_weight, ("ctx", "fsdp"), axis=0, tiled=True),
        lax.all_gather(value_weight, ("ctx", "fsdp"), axis=0, tiled=True),
        lax.all_gather(query_bias, ("ctx", "fsdp"), axis=0, tiled=True),
        lax.all_gather(key_bias, ("ctx", "fsdp"), axis=0, tiled=True),
        lax.all_gather(value_bias, ("ctx", "fsdp"), axis=0, tiled=True),
        lax.all_gather(output_weight, ("ctx", "fsdp"), axis=0, tiled=True),
    )
    grad_branch = grad_mid.astype(jnp.bfloat16)
    term_output = outer_sum(attn_low, grad_branch)
    grad_attn = (
        times_back(grad_branch, w_output).reshape(seq_rows, HEADS, HEAD).astype(jnp.bfloat16)
    )
    delta = jnp.sum(grad_attn.astype(jnp.float32) * attn_rows, axis=-1).T

    def attend_back(query_grad, key_block, value_block, key_grad, value_grad, source):
        mask = visible(query_glob, starts, source * seq_rows + offsets)[None]
        scores = head_scores(queries, key_block) * scale
        probs = jnp.where(mask, jnp.exp(scores - log_total[..., None]), 0.0)
        grad_probs_attn = jnp.einsum(
            "qhd,khd->hqk", grad_attn, value_block, preferred_element_type=jnp.float32
        )
        grad_scores = (probs * (grad_probs_attn - delta[..., None])).astype(jnp.bfloat16)
        query_grad = (
            query_grad
            + jnp.einsum("hqk,khd->qhd", grad_scores, key_block, preferred_element_type=jnp.float32)
            * scale
        )
        key_grad = (
            key_grad
            + jnp.einsum("hqk,qhd->khd", grad_scores, queries, preferred_element_type=jnp.float32)
            * scale
        )
        value_grad = value_grad + jnp.einsum(
            "hqk,qhd->khd",
            probs.astype(jnp.bfloat16),
            grad_attn,
            preferred_element_type=jnp.float32,
        )
        return (query_grad, key_grad, value_grad)

    def back_step(step, carry):
        query_grad, key_block, value_block, key_grad, value_grad = carry
        source = (cycle_index - step) % cycle_size
        query_grad, key_grad, value_grad = attend_back(
            query_grad, key_block, value_block, key_grad, value_grad, source
        )
        key_block, value_block = from_behind((key_block, value_block), "ctx", 1)
        key_grad, value_grad = (
            shifted(key_grad.astype(jnp.bfloat16), "ctx", 1).astype(key_grad.dtype),
            shifted(value_grad.astype(jnp.bfloat16), "ctx", 1).astype(value_grad.dtype),
        )
        return (query_grad, key_block, value_block, key_grad, value_grad)

    zeros = jnp.zeros((seq_rows, HEADS, HEAD), jnp.float32)
    query_grad, key_home, value_home, key_grad, value_grad = lax.fori_loop(
        0, cycle_size, back_step, (zeros, keys, values, zeros, zeros)
    )
    grad_query_pre = (
        rotate_back(query_grad, cosine, sine).reshape(seq_rows, width).astype(jnp.bfloat16)
    )
    grad_key_pre = rotate_back(key_grad, cosine, sine).reshape(seq_rows, width).astype(jnp.bfloat16)
    grad_value_pre = value_grad.reshape(seq_rows, width).astype(jnp.bfloat16)
    term_query = outer_sum(normed, grad_query_pre)
    term_key = outer_sum(normed, grad_key_pre)
    term_value = outer_sum(normed, grad_value_pre)
    term_query_bias = jnp.sum(grad_query_pre.astype(jnp.float32), axis=0)
    term_key_bias = jnp.sum(grad_key_pre.astype(jnp.float32), axis=0)
    term_value_bias = jnp.sum(grad_value_pre.astype(jnp.float32), axis=0)
    grad_normed = (
        times_back(grad_query_pre, w_query)
        + times_back(grad_key_pre, w_key)
        + times_back(grad_value_pre, w_value)
    )
    term_gain_in = jnp.sum(grad_normed * unit_in, axis=0)
    scaled_in = grad_normed * gain_in.astype(jnp.float32)
    grad_states = grad_mid + scale_in * (
        scaled_in - unit_in * jnp.mean(scaled_in * unit_in, axis=-1, keepdims=True)
    )
    (
        grad_attn_gain,
        grad_query_weight,
        grad_key_weight,
        grad_value_weight,
        grad_query_bias,
        grad_key_bias,
        grad_value_bias,
        grad_output_weight,
    ) = (
        lax.psum_scatter(term_gain_in, ("ctx", "fsdp"), scatter_dimension=0, tiled=True),
        lax.psum_scatter(term_query, ("ctx", "fsdp"), scatter_dimension=0, tiled=True),
        lax.psum_scatter(term_key, ("ctx", "fsdp"), scatter_dimension=0, tiled=True),
        lax.psum_scatter(term_value, ("ctx", "fsdp"), scatter_dimension=0, tiled=True),
        lax.psum_scatter(term_query_bias, ("ctx", "fsdp"), scatter_dimension=0, tiled=True),
        lax.psum_scatter(term_key_bias, ("ctx", "fsdp"), scatter_dimension=0, tiled=True),
        lax.psum_scatter(term_value_bias, ("ctx", "fsdp"), scatter_dimension=0, tiled=True),
        lax.psum_scatter(term_output, ("ctx", "fsdp"), scatter_dimension=0, tiled=True),
    )
    return (
        result.astype(jnp.bfloat16)[None],
        grad_states[None],
        grad_attn_gain,
        grad_query_weight,
        grad_key_weight,
        grad_value_weight,
        grad_query_bias,
        grad_key_bias,
        grad_value_bias,
        grad_output_weight,
        grad_ffn_gain,
        grad_router_weight,
        grad_expert_gate,
        grad_expert_up,
        grad_expert_down,
        grad_shared_gate,
        grad_shared_up,
        grad_shared_down,
        grad_shared_sigmoid,
    )


def solution(mesh):
    return jax.shard_map(
        body,
        mesh=mesh,
        in_specs=(
            P("fsdp", "ctx", None),
            P("fsdp", "ctx"),
            P("fsdp", "ctx", None),
            P("fsdp", "ctx", None),
            P(("ctx", "fsdp")),
            P(("ctx", "fsdp"), None),
            P(("ctx", "fsdp"), None),
            P(("ctx", "fsdp"), None),
            P(("ctx", "fsdp")),
            P(("ctx", "fsdp")),
            P(("ctx", "fsdp")),
            P(("ctx", "fsdp"), None),
            P(("ctx", "fsdp")),
            P(("ctx", "fsdp"), None),
            P("ctx", "fsdp", None),
            P("ctx", "fsdp", None),
            P("ctx", "fsdp", None),
            P(("ctx", "fsdp"), None),
            P(("ctx", "fsdp"), None),
            P(("ctx", "fsdp"), None),
            P(("ctx", "fsdp")),
        ),
        out_specs=(
            P("fsdp", "ctx", None),
            P("fsdp", "ctx", None),
            P(("ctx", "fsdp")),
            P(("ctx", "fsdp"), None),
            P(("ctx", "fsdp"), None),
            P(("ctx", "fsdp"), None),
            P(("ctx", "fsdp")),
            P(("ctx", "fsdp")),
            P(("ctx", "fsdp")),
            P(("ctx", "fsdp"), None),
            P(("ctx", "fsdp")),
            P(("ctx", "fsdp"), None),
            P("ctx", "fsdp", None),
            P("ctx", "fsdp", None),
            P("ctx", "fsdp", None),
            P(("ctx", "fsdp"), None),
            P(("ctx", "fsdp"), None),
            P(("ctx", "fsdp"), None),
            P(("ctx", "fsdp")),
        ),
        check_vma=False,
    )
```

profile of v0, /device:TPU:0, one launch (start us, length us, event | category | flops | bytes accessed | tf_op | source)
XLA Modules:
  0.0 5971.2 jit_solution(15517215233291152446)
XLA Ops:
  16.0 42.9 all-reduce.13
  60.6 68.1 %all-gather = bf16[32,64,8]{1,2,0:T(8,128)(2,1)S(1)} all-gather(bf16[1,64,8]{1,2,0:T(8,128)(2,1)S(1)} %bitcast.327), channel_id=1, replica_groups=mesh['ctx'=8,'fsdp'=4] {'ctx','fsdp'}, dimensions={0}, use_global_device_ids=true | all-gather | bytes 33792 | tf_op jit(solution)/shard_map/all_gather | solution.py:202
  135.6 35.0 all-gather.12.cloned.1.call-done
  181.0 68.7 %all-gather.16.cloned.1.call-done = bf16[2048,2048]{1,0:T(8,128)(2,1)} async-done(((bf16[64,2048]{1,0:T(8,128)(2,1)}), bf16[2048,2048]{1,0:T(8,128)(2,1)}) %all-gather.16.cloned.1.call-update) | async-done | bytes 8388624 | tf_op jit(solution)/shard_map/all_gather | solution.py:139
  259.7 132.1 %while.48 = (s32[]{:T(128)}, f32[16,128]{1,0:T(8,128)S(1)}, f32[16,128]{1,0:T(8,128)S(1)}, f32[128,16,128]{2,0,1:T(8,128)S(1)}, bf16[128,16,128]{2,0,1:T(8,128)(...) while((s32[]{:T(128)}, f32[16,128]{1,0:T(8,128)S(1)}, ...), condition=%wide.region_6.7_spmd.clone, body=%wide.region_3.6_spmd.clone.sunk | while | flops 137156880 | bytes 13306730 | solution.py:192
  268.9 10.3 collective-permute-start
  286.8 13.1 collective-permute-start
  307.4 23.2 collective-permute-start
  338.7 9.8 collective-permute-start
  356.0 10.3 collective-permute-start
  373.9 10.3 collective-permute-start
  402.8 16.7 all-to-all-start.2
  423.0 45.8 all-to-all-done.2
  473.4 12.0 fusion.34
  485.3 65.2 %all-gather.22.cloned.1.call-done = bf16[1,2048,1408]{2,1,0:T(8,128)(2,1)} async-done(((bf16[1,512,1408]{2,1,0:T(8,128)(2,1)}), bf16[1,2048,1408]{2,1,0:T(8,128)(2,1)}) %all-gather.22.cloned.1.call-update) | async-done | bytes 5767184 | tf_op jit(solution)/shard_map/all_gather | solution.py:236
  550.6 11.6 fusion.40
  562.2 95.0 %all-gather.20.cloned.1.call-done = bf16[1,2048,1408]{2,1,0:T(8,128)(2,1)} async-done(((bf16[1,512,1408]{2,1,0:T(8,128)(2,1)}), bf16[1,2048,1408]{2,1,0:T(8,128)(2,1)}) %all-gather.20.cloned.1.call-update) | async-done | bytes 5767184 | tf_op jit(solution)/shard_map/all_gather | solution.py:235
  657.2 16.4 multiply_convert_fusion.1
  673.6 9.8 fusion.47
  683.4 74.5 %all_to_all.20 = bf16[8,128,2048]{2,1,0:T(8,128)(2,1)S(1)} all-to-all(bf16[8,128,2048]{2,1,0:T(8,128)(2,1)S(1)} %bitcast.317), channel_id=1, replica_groups=mesh['ctx'=8,'fsdp'=4] {'ctx'}, dimensions={0} | all-to-all | bytes 8388608 | tf_op jit(solution)/shard_map/all_to_all | solution.py:249
  762.9 11.0 fusion.31
  773.9 11.3 fusion.32
  785.3 9.8 fusion.38
  795.1 11.0 add_convert_fusion
  811.7 10.8 fusion.33
  823.1 41.9 all-to-all-done.3
  869.0 12.9 fusion.130
  881.9 100.4 %all-gather.28.cloned.1.call-done = bf16[2048,5632]{1,0:T(8,128)(2,1)} async-done(((bf16[64,5632]{1,0:T(8,128)(2,1)}), bf16[2048,5632]{1,0:T(8,128)(2,1)}) %all-gather.28.cloned.1.call-update) | async-done | bytes 23068688 | tf_op jit(solution)/shard_map/all_gather | solution.py:204
  982.4 12.3 fusion.131
  994.7 133.2 %all-gather.30.cloned.1.call-done = bf16[5632,2048]{1,0:T(8,128)(2,1)} async-done(((bf16[176,2048]{1,0:T(8,128)(2,1)}), bf16[5632,2048]{1,0:T(8,128)(2,1)}) %all-gather.30.cloned.1.call-update) | async-done | bytes 23068688 | tf_op jit(solution)/shard_map/all_gather | solution.py:205
  1127.8 14.9 multiply_convert_fusion.4
  1142.8 13.2 multiply_reduce_fusion.5
  1156.0 11.8 fusion.133
  1167.9 13.3 convolution_add_fusion.1
  1194.7 241.1 %while.49 = (s32[]{:T(128)}, f32[128,16,128]{2,0,1:T(8,128)}, bf16[128,16,128]{2,0,1:T(8,128)(2,1)}, bf16[128,16,128]{2,0,1:T(8,128)(2,1)}, f32[128,16,128]{2,0,...) while((s32[]{:T(128)}, f32[128,16,128]{2,0,1:T(8,128)}, ...), condition=%wide.region_23.24_spmd.clone, body=%wide.region_22.23_spmd.clone.sunk | while | flops 340574464 | bytes 35703828 | solution.py:427
  1251.9 8.9 collective-permute-start.4
  1481.9 18.4 fusion.136
  1501.7 18.1 fusion.137
  1521.1 19.1 fusion.101
  1548.1 27.8 reduce-scatter.26.cloned.1.call-done
  1593.4 45.8 all-reduce.12
  1645.3 299.2 %reduce-scatter.14.cloned.1.call-done = f32[64,2048]{1,0:T(8,128)} async-done(((f32[2048,2048]{1,0:T(8,128)}), f32[64,2048]{1,0:T(8,128)}) %reduce-scatter.14.cloned.1.call-update) | async-done | bytes 524304 | tf_op jit(solution)/shard_map/reduce_scatter | solution.py:462
  1944.4 365.0 %reduce-scatter.16.cloned.1.call-done = f32[64,2048]{1,0:T(8,128)} async-done(((f32[2048,2048]{1,0:T(8,128)}), f32[64,2048]{1,0:T(8,128)}) %reduce-scatter.16.cloned.1.call-update) | async-done | bytes 524304 | tf_op jit(solution)/shard_map/reduce_scatter | solution.py:463
  2309.5 365.0 %reduce-scatter.18.cloned.1.call-done = f32[64,2048]{1,0:T(8,128)} async-done(((f32[2048,2048]{1,0:T(8,128)}), f32[64,2048]{1,0:T(8,128)}) %reduce-scatter.18.cloned.1.call-update) | async-done | bytes 524304 | tf_op jit(solution)/shard_map/reduce_scatter | solution.py:464
  2674.5 365.0 %reduce-scatter.20.cloned.1.call-done = f32[64,2048]{1,0:T(8,128)} async-done(((f32[2048,2048]{1,0:T(8,128)}), f32[64,2048]{1,0:T(8,128)}) %reduce-scatter.20.cloned.1.call-update) | async-done | bytes 524304 | tf_op jit(solution)/shard_map/reduce_scatter | solution.py:468
  3039.5 973.3 %reduce-scatter.28.cloned.1.call-done = f32[64,5632]{1,0:T(8,128)} async-done(((f32[2048,5632]{1,0:T(8,128)}), f32[64,5632]{1,0:T(8,128)}) %reduce-scatter.28.cloned.1.call-update) | async-done | bytes 1441808 | tf_op jit(solution)/shard_map/reduce_scatter | solution.py:365
  4012.8 975.6 %reduce-scatter.30.cloned.1.call-done = f32[64,5632]{1,0:T(8,128)} async-done(((f32[2048,5632]{1,0:T(8,128)}), f32[64,5632]{1,0:T(8,128)}) %reduce-scatter.30.cloned.1.call-update) | async-done | bytes 1441808 | tf_op jit(solution)/shard_map/reduce_scatter | solution.py:366
  4988.4 975.8 %reduce-scatter.32.cloned.1.call-done = f32[176,2048]{1,0:T(8,128)} async-done(((f32[5632,2048]{1,0:T(8,128)}), f32[176,2048]{1,0:T(8,128)}) %reduce-scatter.32.cloned.1.call-update) | async-done | bytes 1441808 | tf_op jit(solution)/shard_map/reduce_scatter | solution.py:367
  (592 shorter events, 450.1 us)
Async XLA Ops:
  7.3 123.5 %all-gather.14.cloned.1.call-start = ((), (), s32[]{:S(2)}) async-start(), calls=%async_computation.16 | async-start | bytes 8650752 | tf_op jit(solution)/shard_map/all_gather | solution.py:138
  8.0 162.7 %all-gather.12.cloned.1.call-start = ((), (), s32[]{:S(2)}) async-start(), calls=%async_computation.15 | async-start | bytes 8650752 | tf_op jit(solution)/shard_map/all_gather | solution.py:137
  8.8 240.9 %all-gather.16.cloned.1.call-start = ((), (), s32[]{:S(2)}) async-start(), calls=%async_computation.17 | async-start | bytes 8650752 | tf_op jit(solution)/shard_map/all_gather | solution.py:139
  9.5 382.9 %all-gather.18.cloned.1.call-start = ((), (), s32[]{:S(2)}) async-start(), calls=%async_computation.18 | async-start | bytes 8650752 | tf_op jit(solution)/shard_map/all_gather | solution.py:143
  10.1 463.2 %all-gather.24.cloned.1.call-start = ((), (), s32[]{:S(2)}) async-start(), calls=%async_computation.21 | async-start | bytes 7208960 | tf_op jit(solution)/shard_map/all_gather | solution.py:237
  10.7 539.9 %all-gather.22.cloned.1.call-start = ((), (), s32[]{:S(2)}) async-start(), calls=%async_computation.20 | async-start | bytes 7208960 | tf_op jit(solution)/shard_map/all_gather | solution.py:236
  11.3 645.9 %all-gather.20.cloned.1.call-start = ((), (), s32[]{:S(2)}) async-start(), calls=%async_computation.19 | async-start | bytes 7208960 | tf_op jit(solution)/shard_map/all_gather | solution.py:235
  12.0 857.0 %all-gather.26.cloned.1.call-start = ((), (), s32[]{:S(2)}) async-start(), calls=%async_computation.22 | async-start | bytes 23789568 | tf_op jit(solution)/shard_map/all_gather | solution.py:203
  12.8 969.6 %all-gather.28.cloned.1.call-start = ((), (), s32[]{:S(2)}) async-start(), calls=%async_computation.23 | async-start | bytes 23789568 | tf_op jit(solution)/shard_map/all_gather | solution.py:204
  13.5 1114.3 %all-gather.30.cloned.1.call-start = ((), (), s32[]{:S(2)}) async-start(), calls=%async_computation.24 | async-start | bytes 23789568 | tf_op jit(solution)/shard_map/all_gather | solution.py:205
  268.9 14.8 collective-permute-start
  286.8 17.5 collective-permute-start
  307.4 27.6 collective-permute-start
  356.0 14.8 collective-permute-start
  402.8 65.9 %all-to-all-start.2 = ((bf16[8,128,2048]{2,1,0:T(8,128)(2,1)}), bf16[8,128,2048]{2,1,0:T(8,128)(2,1)}, u32[]{:S(2)}, u32[]{:S(2)}) async-start(bf16[8,128,2048]{2,1,0:T(8,128)(2,1)} %bitcast.315), calls=%async_computation.2 | async-start | bytes 8388608 | tf_op jit(solution)/shard_map/all_to_all | solution.py:275
  468.7 81.8 %all-to-all-start = ((bf16[8,128,2048]{2,1,0:T(8,128)(2,1)}), bf16[8,128,2048]{2,1,0:T(8,128)(2,1)}, u32[]{:S(2)}, u32[]{:S(2)}) async-start(bf16[8,128,2048]{2,1,0:T(8,128)(2,1)} %bitcast.302), calls=%async_computation | async-start | bytes 8388608 | tf_op jit(solution)/shard_map/all_to_all | solution.py:227
  473.3 1067.0 %reduce-scatter.34.cloned.1.call-start = ((), (), s32[]{:S(2)}) async-start(), calls=%async_computation.35 | async-start | bytes 1081344
  762.8 778.9 %reduce-scatter.22.cloned.1.call-start = ((), (), s32[]{:S(2)}) async-start(), calls=%async_computation.29 | async-start | bytes 7208960 | tf_op jit(solution)/shard_map/reduce_scatter | solution.py:315
  773.9 771.0 %reduce-scatter.24.cloned.1.call-start = ((), (), s32[]{:S(2)}) async-start(), calls=%async_computation.30 | async-start | bytes 7208960 | tf_op jit(solution)/shard_map/reduce_scatter | solution.py:318
  806.1 59.0 all-to-all-start.3
  810.8 765.2 %reduce-scatter.26.cloned.1.call-start = ((), (), s32[]{:S(2)}) async-start(), calls=%async_computation.31 | async-start | bytes 7208960 | tf_op jit(solution)/shard_map/reduce_scatter | solution.py:321
  822.6 1121.8 %reduce-scatter.14.cloned.1.call-start = ((), (), s32[]{:S(2)}) async-start(), calls=%async_computation.25 | async-start | bytes 17301504 | tf_op jit(solution)/shard_map/reduce_scatter | solution.py:462
  1201.9 15.5 collective-permute-start.2
  1222.0 21.1 collective-permute-start.4
  1251.9 23.4 collective-permute-start.4
  1262.0 15.5 collective-permute-start.5
  1264.5 15.1 collective-permute-start.2
  1284.2 22.4 collective-permute-start.4
  1292.3 16.4 collective-permute-start.5
  1294.9 16.0 collective-permute-start.2
  1315.4 22.4 collective-permute-start.4
  1322.6 17.3 collective-permute-start.5
  1325.2 16.9 collective-permute-start.2
  1346.6 22.4 collective-permute-start.4
  1352.9 18.2 collective-permute-start.5
  1355.6 17.7 collective-permute-start.2
  1378.0 22.3 collective-permute-start.4
  1383.3 19.1 collective-permute-start.5
  1385.9 18.7 collective-permute-start.2
  1409.1 22.4 collective-permute-start.4
  1413.6 20.1 collective-permute-start.5
  1416.2 19.6 collective-permute-start.2
  1450.3 859.1 %reduce-scatter.16.cloned.1.call-start = ((), (), s32[]{:S(2)}) async-start(), calls=%async_computation.26 | async-start | bytes 17301504 | tf_op jit(solution)/shard_map/reduce_scatter | solution.py:463
  1460.4 1214.0 %reduce-scatter.18.cloned.1.call-start = ((), (), s32[]{:S(2)}) async-start(), calls=%async_computation.27 | async-start | bytes 17301504 | tf_op jit(solution)/shard_map/reduce_scatter | solution.py:464
  1470.2 1569.3 %reduce-scatter.20.cloned.1.call-start = ((), (), s32[]{:S(2)}) async-start(), calls=%async_computation.28 | async-start | bytes 17301504 | tf_op jit(solution)/shard_map/reduce_scatter | solution.py:468
  1480.3 2532.5 %reduce-scatter.28.cloned.1.call-start = ((), (), s32[]{:S(2)}) async-start(), calls=%async_computation.32 | async-start | bytes 47579136 | tf_op jit(solution)/shard_map/reduce_scatter | solution.py:365
  1500.4 3488.0 %reduce-scatter.30.cloned.1.call-start = ((), (), s32[]{:S(2)}) async-start(), calls=%async_computation.33 | async-start | bytes 47579136 | tf_op jit(solution)/shard_map/reduce_scatter | solution.py:366
  1519.8 4444.4 %reduce-scatter.32.cloned.1.call-start = ((), (), s32[]{:S(2)}) async-start(), calls=%async_computation.34 | async-start | bytes 47579136 | tf_op jit(solution)/shard_map/reduce_scatter | solution.py:367
  (106 other events, 2764.4 us)
Sparse Core Ops, SparseCore 0:
  11.0 80.4 all-gather.13
  94.5 76.1 all-gather.11
  173.6 75.9 all-gather.15
  252.4 84.6 all-gather.17
  338.6 105.4 all-gather.23
  445.5 104.9 all-gather.21
  552.1 104.9 all-gather.19
  660.0 163.7 all-gather.25
  826.7 155.6 all-gather.27
  985.0 142.7 all-gather.29
  1130.1 134.3 reduce-scatter.33
  1266.8 98.8 reduce-scatter.21
  1368.1 102.7 reduce-scatter.23
  1473.2 102.7 reduce-scatter.25
  1578.8 365.5 reduce-scatter.13
  1947.3 362.1 reduce-scatter.15
  2312.3 362.1 reduce-scatter.17
  2677.3 362.1 reduce-scatter.19
  3042.5 970.2 reduce-scatter.27
  4015.6 972.7 reduce-scatter.29
  4991.4 972.7 reduce-scatter.31
where the time goes:
time: 5980 us; the launch traced here: 5970 us
  waiting for transfers between devices  4940 us (83%)
  matrix products  386 us (6%)
  starting transfers between devices  275 us (5%)
  blocking collectives  231 us (4%)
  other arithmetic  64.1 us (1%)
    reduce_scatter x1, waiting for transfers between devices, body(): lax.psum_scatter(term_shared_down, ('ctx', 'fsdp'), scatter_dimension=0,...  976 us
    reduce_scatter x1, waiting for transfers between devices, body(): lax.psum_scatter(term_shared_up, ('ctx', 'fsdp'), scatter_dimension=0, ti...  976 us
    reduce_scatter x1, waiting for transfers between devices, body(): lax.psum_scatter(term_shared_gate, ('ctx', 'fsdp'), scatter_dimension=0,...  973 us
    reduce_scatter x1, waiting for transfers between devices, body(): lax.psum_scatter(term_output, ('ctx', 'fsdp'), scatter_dimension=0, tiled...  365 us
    reduce_scatter x1, waiting for transfers between devices, body(): lax.psum_scatter(term_key, ('ctx', 'fsdp'), scatter_dimension=0, tiled=True)  365 us
    reduce_scatter x1, waiting for transfers between devices, body(): lax.psum_scatter(term_value, ('ctx', 'fsdp'), scatter_dimension=0, tiled=...  365 us
    reduce_scatter x1, waiting for transfers between devices, body(): lax.psum_scatter(term_query, ('ctx', 'fsdp'), scatter_dimension=0, tiled=...  299 us
    ppermute x30, starting transfers between devices, from_behind(): lax.ppermute(value, axis, [(source, source + steps) for source in range(l...  185 us
  transfers between devices with their start and end apart: 70, of which 18 were waited for; matrix products, arithmetic and copies ran while one was open for 8% of the time, Pallas kernels for 0%

commit v1 on v0

v1 whole, which is shorter than its diff:
```python
import functools
import math

import jax
import jax.numpy as jnp
from jax import lax
from jax.experimental import pallas as pl
from jax.experimental.pallas import tpu as pltpu
from jax.sharding import PartitionSpec as P

HEADS = 16
HEAD = 128
EPS = 1e-06
ROPE_BASE = 1000000.0
MASKED = -1e30
BLOCK = 1024
BOTH = ("ctx", "fsdp")
BF16 = jnp.bfloat16
F32 = jnp.float32


PLANE, LINE = 8, 4
LANES = 128
HBM = pl.BlockSpec(memory_space=pl.ANY)
VMEM = pl.BlockSpec(memory_space=pltpu.VMEM)


class Place:
    def __init__(self):
        self.c = lax.axis_index("ctx")
        self.z = lax.axis_index("fsdp")
        self.core = self.c % 2
        self.x = (self.c // 2) % 2
        self.y = self.c // 4
        self.twin = self.c + 1 - 2 * self.core
        self.across = self.c + 2 - 4 * self.x
        self.along = self.c + 4 - 8 * self.y
        self.far = self.across + 4 - 8 * self.y
        self.upper = self.z // 2
        self.depth = self.z + self.upper * (3 - 2 * self.z)
        self.near = self.z + 1 - 2 * (self.z % 2)
        self.middle = 3 - self.z

    def mirrored(self, number):
        return number + self.upper * (3 - 2 * number)

    def plane(self, c):
        return (c, self.z)

    def line(self, z):
        return (self.c, z)

    def on_line(self):
        return [(self.z + step) % LINE for step in (2, 1, 3)]


class Wire:
    def __init__(self, send, recv):
        self.send, self.recv, self.used, self.open = send, recv, 0, []

    def copy(self, source, target, device, arrival=None):
        number = self.used
        self.used += 1
        return pltpu.make_async_remote_copy(
            src_ref=source,
            dst_ref=target,
            send_sem=self.send.at[number],
            recv_sem=self.recv.at[number if arrival is None else arrival],
            device_id=device,
            device_id_type=pl.DeviceIdType.MESH,
        )

    def later(self, source, target, device, arrival=None):
        copy = self.copy(source, target, device, arrival)
        self.open.append(copy)
        return copy

    def push(self, source, target, device):
        copy = self.later(source, target, device)
        copy.start()
        return copy

    def close(self):
        for copy in self.open:
            copy.wait_send()


def greet(devices):
    barrier = pltpu.get_barrier_semaphore()
    for device in devices:
        pl.semaphore_signal(
            barrier, inc=1, device_id=device, device_id_type=pl.DeviceIdType.MESH
        )
    pl.semaphore_wait(barrier, len(devices))


class PlaneGather:
    def __init__(self, wire, here, at, source=None):
        source = at(here.c) if source is None else source
        to_x, to_y = here.plane(here.across), here.plane(here.along)
        to_twin = here.plane(here.twin)
        x_block, y_block, far_block = at(here.across), at(here.along), at(here.far)
        half = x_block.shape[0] // 2
        high, low = x_block.at[pl.ds(half, half)], y_block.at[pl.ds(0, half)]
        self.from_x = wire.later(source, at(here.c), to_x)
        self.from_y = wire.later(source, at(here.c), to_y)
        self.far_y = wire.later(high, high, to_y)
        self.far_x = wire.later(low, low, to_x)
        blocks = [(source, at(here.c))] + [(b, b) for b in (x_block, y_block, far_block)]
        self.twins = [wire.later(block, target, to_twin) for block, target in blocks]

    def first(self):
        self.from_x.start()
        self.from_y.start()
        self.twins[0].start()
        return self

    def second(self):
        self.from_x.wait_recv()
        self.far_y.start()
        self.twins[1].start()
        self.from_y.wait_recv()
        self.far_x.start()
        self.twins[2].start()

    def third(self):
        self.far_x.wait_recv()
        self.far_y.wait_recv()
        self.twins[3].start()

    def finish(self):
        for copy in self.twins:
            copy.wait_recv()


PLANE_GATHER_COPIES = 8


class LineGather:
    def __init__(self, wire, here, at, source=None):
        self.wire, self.here, self.at = wire, here, at
        source = at(here.z) if source is None else source
        self.one = wire.push(source, at(here.z), here.line(here.near))
        inner = here.depth == 1
        middle, near = here.line(here.middle), here.line(here.near)
        own, mine = source, at(here.z)
        end, two, three = at(here.mirrored(0)), at(here.mirrored(2)), at(here.mirrored(3))
        self.inner = inner
        self.two_in = wire.copy(own, mine, middle)
        self.three_in = wire.copy(end, end, middle)
        self.two_out = wire.copy(two, two, near)
        self.three_out = wire.copy(three, three, near)

        @pl.when(inner)
        def _():
            self.two_in.start()

    def first(self):
        self.one.wait_recv()
        pl.when(self.inner)(self.three_in.start)

    def second(self):
        @pl.when(self.inner)
        def _():
            self.two_in.wait_recv()
            self.two_out.start()

        @pl.when(self.here.depth == 0)
        def _():
            self.two_out.wait_recv()

    def third(self):
        @pl.when(self.inner)
        def _():
            self.three_in.wait_recv()
            self.three_out.start()

        @pl.when(self.here.depth == 0)
        def _():
            self.three_out.wait_recv()

    def order(self):
        here = self.here
        return [here.z, here.near, here.mirrored(2), here.mirrored(3)]

    def finish(self):
        @pl.when(self.inner)
        def _():
            for copy in (self.two_in, self.three_in, self.two_out, self.three_out):
                copy.wait_send()


LINE_GATHER_COPIES = 5


def add_into(total, part):
    rows = total.shape[0]
    step = min(rows, 32)

    @pl.loop(0, rows // step)
    def _(i):
        at = pl.ds(pl.multiple_of(i * step, step), step)
        total[at] = total[at] + part[at]


class PlaneScatter:
    def __init__(self, wire, here, parts, room):
        self.here, self.parts, self.room = here, parts, room
        arrived, one_x, one_y, two_x, two_y = room
        self.half = arrived.shape[1] // 2
        to_x, to_y = here.plane(here.across), here.plane(here.along)
        self.twin = wire.later(parts.at[:, 1 - here.core], arrived, here.plane(here.twin))
        self.from_x = [
            wire.later(self.block(y, 1 - here.x, 0), one_x.at[y], to_x) for y in range(2)
        ]
        self.from_y = [
            wire.later(self.block(1 - here.y, x, 1), one_y.at[x], to_y) for x in range(2)
        ]
        self.last_y = wire.later(self.block(1 - here.y, here.x, 0), two_y, to_y)
        self.last_x = wire.later(self.block(here.y, 1 - here.x, 1), two_x, to_x)

    def block(self, y, x, half=None):
        if half is None:
            return self.parts.at[y * 2 + x, self.here.core]
        return self.parts.at[y * 2 + x, self.here.core, pl.ds(half * self.half, self.half)]

    def begin(self):
        self.twin.start()

    def first(self):
        self.twin.wait_recv()
        for i in range(4):
            add_into(self.parts.at[i, self.here.core], self.room[0].at[i])
        for copy in self.from_x + self.from_y:
            copy.start()

    def second(self):
        here, one_x, one_y = self.here, self.room[1], self.room[2]
        for copy in self.from_x:
            copy.wait_recv()
        add_into(self.block(1 - here.y, here.x, 0), one_x.at[1 - here.y])
        self.last_y.start()
        for copy in self.from_y:
            copy.wait_recv()
        add_into(self.block(here.y, 1 - here.x, 1), one_y.at[1 - here.x])
        self.last_x.start()
        add_into(self.block(here.y, here.x, 0), one_x.at[here.y])
        add_into(self.block(here.y, here.x, 1), one_y.at[here.x])

    def third(self):
        here, two_x, two_y = self.here, self.room[3], self.room[4]
        self.last_y.wait_recv()
        add_into(self.block(here.y, here.x, 0), two_y)
        self.last_x.wait_recv()
        add_into(self.block(here.y, here.x, 1), two_x)

    def mine(self):
        return self.block(self.here.y, self.here.x)


PLANE_SCATTER_COPIES = 7


class LineScatter:
    def __init__(self, wire, here, blocks, room):
        self.here, self.blocks = here, blocks
        near, middle = here.line(here.near), here.line(here.middle)
        self.ends, self.mids = room
        own = self.blocks
        self.out = [wire.copy(own[i], self.ends.at[k], near) for k, i in enumerate((2, 3, 1))]
        self.over = [wire.copy(own[i], self.mids.at[k], middle) for k, i in enumerate((2, 3))]
        self.home = wire.copy(own[0], self.ends.at[0], near)

    def begin(self):
        @pl.when(self.here.depth == 0)
        def _():
            for copy in self.out:
                copy.start()

    def first(self):
        @pl.when(self.here.depth == 1)
        def _():
            for k in range(2):
                self.out[k].wait_recv()
                add_into(self.blocks[2 + k], self.ends.at[k])
                self.over[k].start()

    def second(self):
        @pl.when(self.here.depth == 1)
        def _():
            self.over[1].wait_recv()
            add_into(self.blocks[0], self.mids.at[1])
            self.home.start()
            self.out[2].wait_recv()
            add_into(self.blocks[1], self.ends.at[2])
            self.over[0].wait_recv()
            add_into(self.blocks[1], self.mids.at[0])

    def third(self):
        @pl.when(self.here.depth == 0)
        def _():
            self.home.wait_recv()
            add_into(self.blocks[0], self.ends.at[0])
            for copy in self.out:
                copy.wait_send()

        @pl.when(self.here.depth == 1)
        def _():
            for copy in self.over + [self.home]:
                copy.wait_send()


LINE_SCATTER_COPIES = 6


def scatter_room(rows, columns, kind):
    half = rows // 2
    return [
        pltpu.VMEM((4, rows, columns), kind),
        pltpu.VMEM((2, half, columns), kind),
        pltpu.VMEM((2, half, columns), kind),
        pltpu.VMEM((half, columns), kind),
        pltpu.VMEM((half, columns), kind),
    ]


def wires(count):
    return [pltpu.SemaphoreType.DMA((count,)), pltpu.SemaphoreType.DMA((count,))]


def call(kernel, number, outs, args, scratch, out_specs=None, in_specs=None, aliases=None):
    return pl.pallas_call(
        kernel,
        out_shape=[jax.ShapeDtypeStruct(shape, kind) for shape, kind in outs],
        in_specs=in_specs or [HBM] * len(args),
        out_specs=out_specs or [HBM] * len(outs),
        scratch_shapes=scratch,
        input_output_aliases=aliases or {},
        compiler_params=pltpu.CompilerParams(
            collective_id=number, has_side_effects=True, vmem_limit_bytes=60 << 20
        ),
    )(*args)


def start_kernel(
    tokens, three, output, small, shared, later, x_out, three_out, output_out, small_out,
    shared_out, later_out, send, recv, local
):
    here, wire = Place(), Wire(send, recv)
    others = [(here.c + step) % PLANE for step in range(1, PLANE)]
    greet([here.plane(c) for c in others] + [here.line(z) for z in here.on_line()])
    small_line = [
        wire.push(small, small_out.at[here.c, here.z], here.line(z)) for z in here.on_line()
    ]
    plane = [
        wire.push(three.at[c], three_out.at[here.c, here.z], here.plane(c)) for c in others
    ]
    mine = [
        pltpu.make_async_copy(small, small_out.at[here.c, here.z], local.at[0]),
        pltpu.make_async_copy(three.at[here.c], three_out.at[here.c, here.z], local.at[1]),
        pltpu.make_async_copy(tokens, x_out.at[here.c], local.at[2]),
        pltpu.make_async_copy(output, output_out.at[here.z], local.at[3]),
        pltpu.make_async_copy(shared.at[here.c], shared_out.at[:, here.c], local.at[4]),
    ]
    for copy in mine:
        copy.start()
    x_plane = PlaneGather(wire, here, lambda c: x_out.at[c], tokens).first()
    for copy in mine:
        copy.wait()
    for copy in small_line + plane:
        copy.wait_recv()
    three_line = LineGather(wire, here, lambda z: three_out.at[:, z])
    output_line = LineGather(wire, here, lambda z: output_out.at[z])
    small_plane = PlaneGather(wire, here, lambda c: small_out.at[c]).first()
    swapped = [
        wire.push(shared.at[c], shared_out.at[:, here.c], here.plane(c)) for c in others
    ]
    x_plane.second()
    small_plane.second()
    x_plane.third()
    small_plane.third()
    three_line.first()
    output_line.first()
    three_line.second()
    output_line.second()
    three_line.third()
    output_line.third()
    x_plane.finish()
    small_plane.finish()
    for copy in swapped:
        copy.wait_recv()
    three_line.finish()
    output_line.finish()
    wire.close()


def start_transfers(tokens, three, output, small, shared, later):
    rows, width = tokens.shape
    _, owned, wide = three.shape
    copies = 3 + 7 + 7 + 2 * PLANE_GATHER_COPIES + 2 * LINE_GATHER_COPIES
    return call(
        start_kernel,
        1,
        [
            ((PLANE, rows, width), BF16),
            ((PLANE, LINE, owned, wide), BF16),
            ((LINE, owned, width), BF16),
            ((PLANE, LINE) + small.shape, BF16),
            ((LINE, PLANE) + shared.shape[2:], BF16),
            (later.shape, later.dtype),
        ],
        [tokens, three, output, small, shared, later],
        wires(copies) + [pltpu.SemaphoreType.DMA((5,))],
        in_specs=[VMEM] * 5 + [HBM],
        aliases={5: 5},
    )


def fold_kernel(parts, shared, out, shared_out, *scratch):
    here, wire = Place(), Wire(scratch[0], scratch[1])
    local = scratch[2]
    greet(
        [here.plane(c) for c in (here.twin, here.across, here.along)]
        + [here.line(z) for z in here.on_line()]
    )
    kept = pltpu.make_async_copy(shared.at[here.z], shared_out.at[:, here.z], local.at[2])
    kept.start()
    moved = [
        wire.push(shared.at[z], shared_out.at[:, here.z], here.line(z)) for z in here.on_line()
    ]
    half = parts.shape[2] // 2
    jobs, loads = [], []
    for i in range(2):
        held, room = scratch[3 + 6 * i], scratch[4 + 6 * i : 9 + 6 * i]
        loads.append(
            pltpu.make_async_copy(parts.at[:, :, pl.ds(i * half, half)], held, local.at[i])
        )
        loads[i].start()
        jobs.append(PlaneScatter(wire, here, held, room))
    for load, job in zip(loads, jobs):
        load.wait()
        job.begin()
    for job in jobs:
        job.first()
    for job in jobs:
        job.second()
    for i, job in enumerate(jobs):
        job.third()
        out[pl.ds(i * half, half)] = job.mine()[...].astype(out.dtype)
    for copy in moved:
        copy.wait_recv()
    kept.wait()
    wire.close()


def held_room(rows, columns, kind):
    return [pltpu.VMEM((4, 2, rows, columns), kind)] + scatter_room(rows, columns, kind)


def fold_plane(parts, shared):
    rows, width = parts.shape[0] // PLANE, parts.shape[1]
    return call(
        fold_kernel,
        3,
        [((rows, width), F32), ((PLANE, LINE) + shared.shape[2:], BF16)],
        [parts.reshape(4, 2, rows, width), shared],
        wires(2 * PLANE_SCATTER_COPIES + 3)
        + [pltpu.SemaphoreType.DMA((3,))]
        + held_room(rows // 2, width, BF16) * 2,
        out_specs=[VMEM, HBM],
    )


STEPS, TILE = 8, 512


def ffn_kernel(
    x, few, g, mixed, shared, routed_down, shared_down, x_out, sum_out, dots_out, out_parts, pre_out, weighted_out,
    send, recv, local, fetch, store, w_both, w_down, few_all, parts, landed, dots_parts, dots_landed,
    x_buf, g_buf, o_buf, p_buf, h_buf, pre_buf, back_buf, by_buf, dot_buf, *rooms
):
    here, wire = Place(), Wire(send, recv)
    rows, width = x.shape
    chunk = 4 * rows
    routed, units = routed_down.shape[0], w_down.shape[0]
    used = routed + shared_down.shape[0]
    few_rows = few.shape[0]
    greet(
        [here.plane(c) for c in (here.twin, here.across, here.along)]
        + [here.line(z) for z in here.on_line()]
    )
    own = pltpu.make_async_copy(x, x_out.at[here.z, here.c], local.at[0])
    own.start()
    own_few = pltpu.make_async_copy(few, few_all.at[here.c, here.z], local.at[1])
    own_few.start()
    part = mixed.shape[2]
    pieces = [
        (mixed.at[z, pl.ds(k * routed, routed)], w_both.at[pl.ds(k * units, routed), pl.ds(z * part, part)])
        for z in range(LINE)
        for k in range(2)
    ]
    pieces += [
        (
            shared.at[pl.ds(k * (used - routed), used - routed)],
            w_both.at[pl.ds(k * units + routed, used - routed)],
        )
        for k in range(2)
    ]
    pieces += [
        (routed_down, w_down.at[pl.ds(0, routed)]),
        (shared_down, w_down.at[pl.ds(routed, used - routed)]),
    ]
    weights = [
        pltpu.make_async_copy(source, target, local.at[2 + i])
        for i, (source, target) in enumerate(pieces)
    ]
    for copy in weights:
        copy.start()
    nothing = jnp.zeros((units - used, width), BF16)
    w_both[pl.ds(used, units - used)] = nothing
    w_both[pl.ds(units + used, units - used)] = nothing
    w_down[pl.ds(used, units - used)] = nothing
    few_line = [
        wire.push(few, few_all.at[here.c, here.z], here.line(z)) for z in here.on_line()
    ]
    line = LineGather(wire, here, lambda z: x_out.at[z, here.c], x)
    order = line.order()
    planes = [
        PlaneGather(
            wire, here, functools.partial(lambda z, c: x_out.at[z, c], order[i]), None if i else x
        )
        for i in range(4)
    ]
    few_plane = PlaneGather(wire, here, lambda c: few_all.at[c])
    jobs = [PlaneScatter(wire, here, parts.at[i], rooms[5 * i : 5 * i + 5]) for i in range(4)]
    dots_jobs = [
        PlaneScatter(wire, here, dots_parts.at[i], rooms[20 + 5 * i : 25 + 5 * i])
        for i in range(4)
    ]
    slots = [None, 0, 1 + here.depth, 2 - here.depth]
    base = wire.used
    arrivals = [
        wire.copy(source.at[0, 0, 0], target.at[slot], here.line(here.near))
        for source, target in ((parts, landed), (dots_parts, dots_landed))
        for slot in range(3)
    ]
    lines = [
        wire.later(job.mine(), target.at[slots[i]], here.line(order[i]), base + 3 * k + slots[i])
        for k, (group, target) in enumerate(((jobs, landed), (dots_jobs, dots_landed)))
        for i, job in enumerate(group)
        if i
    ]
    planes[0].first()
    own.wait()
    own_few.wait()
    for copy in few_line:
        copy.wait_recv()
    few_plane.first()

    def where(step):
        group, half = step // 2, step % 2
        late = group // 2
        number = (here.depth + group) % 2 * (1 - late) + group * late
        return group, here.mirrored(number), (here.y + half) % 2

    def loads(step):
        _, z, y = where(step)
        at = pl.ds(4 * y, 4)
        return [
            pltpu.make_async_copy(x_out.at[z, at], x_buf, fetch.at[0]),
            pltpu.make_async_copy(g.at[z, at], g_buf, fetch.at[1]),
        ]

    def stores(step):
        _, z, y = where(step)
        at = pl.ds(4 * y, 4)
        return [
            pltpu.make_async_copy(o_buf, out_parts.at[z, pl.ds(2 * y, 2)], store.at[0]),
            pltpu.make_async_copy(p_buf, pre_out.at[z, at], store.at[1]),
            pltpu.make_async_copy(h_buf, weighted_out.at[z, at], store.at[2]),
        ]

    def scatter(i, phase):
        for job in (jobs[i], dots_jobs[i]):
            getattr(job, phase)()
        if phase == "third" and i:
            lines[i - 1].start()
            lines[3 + i - 1].start()

    def arrived(step):
        for chip in (0, 1):
            planes[step // 2].twins[step % 2 * 2 + chip].wait_recv()

    def begin(i):
        return functools.partial(scatter, i, "begin")

    def first(i):
        return functools.partial(scatter, i, "first")

    def second(i):
        return functools.partial(scatter, i, "second")

    def third(i):
        return functools.partial(scatter, i, "third")

    before = [
        [few_plane.second, few_plane.third, few_plane.finish, planes[0].third, planes[1].second],
        [line.second, planes[2].first, planes[1].third],
        [line.third, planes[3].first, planes[2].second, begin(0)],
        [planes[2].third, planes[3].second, first(0)],
        [planes[3].third, second(0), begin(1)],
        [third(0), first(1)],
        [second(1), begin(2)],
        [third(1), first(2)],
    ]
    after = [begin(3), second(2), first(3), third(2), second(3), third(3)]

    planes[0].second()
    line.first()
    planes[1].first()
    arrived(0)
    for copy in loads(0):
        copy.start()
    for copy in weights:
        copy.wait()

    @pl.loop(0, STEPS)
    def _(step):
        for number in range(STEPS):

            @pl.when(step == number)
            def _():
                for action in before[number]:
                    action()
                if number + 1 < STEPS:
                    arrived(number + 1)

        group, z, y = where(step)
        for b in range(4):
            block = few_all[4 * y + b, z]
            block = jnp.concatenate([block, jnp.zeros((LANES - few_rows, LANES), F32)], axis=0)
            by_buf[pl.ds(b * rows, rows)] = block.T
        for copy in loads(step):
            copy.wait()
        pre_buf[...] = times_back(x_buf[...].reshape(chunk, width), w_both[...])
        back_buf[...] = times_back(g_buf[...].reshape(chunk, width), w_down[...])

        @pl.when(step + 1 < STEPS)
        def _():
            for copy in loads(step + 1):
                copy.start()

        @pl.when(step >= 1)
        def _():
            for copy in stores(step - 1):
                copy.wait()

        size = 32

        @pl.loop(0, chunk // size)
        def _(i):
            at = pl.ds(pl.multiple_of(i * size, size), size)
            gate_pre, up_pre = pre_buf[at, :units], pre_buf[at, units:]
            back = back_buf[at]
            lane = lax.broadcasted_iota(jnp.int32, (size, LANES), 1)
            factor = by_buf[at]
            by_route = jnp.sum(jnp.where(lane == here.c, factor, 0.0), axis=1, keepdims=True)
            by_switch = jnp.sum(jnp.where(lane == PLANE, factor, 0.0), axis=1, keepdims=True)
            is_routed = lax.broadcasted_iota(jnp.int32, (size, units), 1) < routed
            by = jnp.where(is_routed, by_route, by_switch)
            sigma = jax.nn.sigmoid(gate_pre)
            act = gate_pre * sigma
            hidden = act * up_pre
            product = hidden * back
            routed_dot = jnp.sum(jnp.where(is_routed, product, 0.0), axis=1, keepdims=True)
            shared_dot = jnp.sum(jnp.where(is_routed, 0.0, product), axis=1, keepdims=True)
            dot_buf[at] = jnp.where(
                lane == here.c, routed_dot, jnp.where(lane == PLANE, shared_dot, 0.0)
            )
            back = back * by
            block, inner = i // (rows // size), i % (rows // size)
            inside = pl.ds(pl.multiple_of(inner * size, size), size)
            h_buf[block, inside] = (hidden * by).astype(BF16)
            slope = sigma * (1.0 + gate_pre * (1.0 - sigma))
            p_buf[block, inside, :units] = (back * up_pre * slope).astype(BF16)
            p_buf[block, inside, units:] = (back * act).astype(BF16)

        for b in range(4):
            dots_parts[group, 2 * y + b // 2, b % 2] = dot_buf[pl.ds(b * rows, rows)].T[:few_rows]

        @pl.loop(0, width // TILE)
        def _(i):
            at = pl.ds(pl.multiple_of(i * TILE, TILE), TILE)
            both = p_buf[...].reshape(chunk, 2 * units)
            tile = dot(both, w_both[:, at]).astype(BF16)
            parts[group, pl.ds(2 * y, 2), :, :, at] = tile.reshape(2, 2, rows, TILE)
            weighted = h_buf[...].reshape(chunk, units)
            tile = dot(weighted, w_down[:, at]).astype(BF16)
            o_buf[:, :, :, at] = tile.reshape(2, 2, rows, TILE)

        for copy in stores(step):
            copy.start()

    for action in after:
        action()
    for copy in stores(STEPS - 1):
        copy.wait()
    for copy in arrivals:
        copy.wait_recv()
    size = 32

    @pl.loop(0, rows // size)
    def _(i):
        at = pl.ds(pl.multiple_of(i * size, size), size)
        value = jobs[0].mine()[at].astype(F32)
        for j in range(3):
            value += landed[j, at].astype(F32)
        sum_out[at] = value

    dots_out[...] = dots_jobs[0].mine()[...] + dots_landed[0] + dots_landed[1] + dots_landed[2]
    line.finish()
    wire.close()


def feed_forward(x, few, g, mixed, shared, routed_down, shared_down, units):
    rows, width = x.shape
    copies = 3 + LINE_GATHER_COPIES + 5 * PLANE_GATHER_COPIES + 8 * PLANE_SCATTER_COPIES + 12
    return call(
        ffn_kernel,
        2,
        [
            ((LINE, PLANE, rows, width), BF16),
            ((rows, width), F32),
            (few.shape, F32),
            ((LINE, 4, 2, rows, width), BF16),
            ((LINE, PLANE, rows, 2 * units), BF16),
            ((LINE, PLANE, rows, units), BF16),
        ],
        [x, few, g.reshape(LINE, PLANE, rows, width), mixed, shared, routed_down, shared_down],
        wires(copies)
        + [
            pltpu.SemaphoreType.DMA((14,)),
            pltpu.SemaphoreType.DMA((2,)),
            pltpu.SemaphoreType.DMA((3,)),
            pltpu.VMEM((2 * units, width), BF16),
            pltpu.VMEM((units, width), BF16),
            pltpu.VMEM((PLANE, LINE) + few.shape, F32),
            pltpu.VMEM((4, 4, 2, rows, width), BF16),
            pltpu.VMEM((3, rows, width), BF16),
            pltpu.VMEM((4, 4, 2) + few.shape, F32),
            pltpu.VMEM((3,) + few.shape, F32),
            pltpu.VMEM((4, rows, width), BF16),
            pltpu.VMEM((4, rows, width), BF16),
            pltpu.VMEM((2, 2, rows, width), BF16),
            pltpu.VMEM((4, rows, 2 * units), BF16),
            pltpu.VMEM((4, rows, units), BF16),
            pltpu.VMEM((4 * rows, 2 * units), F32),
            pltpu.VMEM((4 * rows, units), F32),
            pltpu.VMEM((4 * rows, LANES), F32),
            pltpu.VMEM((4 * rows, LANES), F32),
        ]
        + scatter_room(rows, width, BF16) * 4
        + scatter_room(few.shape[0], LANES, F32) * 4,
        out_specs=[HBM, VMEM, VMEM, HBM, HBM, HBM],
        in_specs=[VMEM, VMEM] + [HBM] * 5,
    )


def fan_kernel(block, shared, out, shared_out, send, recv, local):
    here, wire = Place(), Wire(send, recv)
    greet(
        [here.plane(c) for c in (here.twin, here.across, here.along)]
        + [here.line(z) for z in here.on_line()]
    )
    half = block.shape[0] // 2
    mine = pltpu.make_async_copy(block, out.at[here.c], local.at[0])
    mine.start()
    jobs = []
    for i in range(2):
        at = pl.ds(i * half, half)
        jobs.append(
            PlaneGather(
                wire, here, functools.partial(lambda at, c: out.at[c, at], at), block.at[at]
            ).first()
        )
    kept = pltpu.make_async_copy(shared.at[:, here.z], shared_out.at[here.z], local.at[1])
    kept.start()
    moved = [
        wire.push(shared.at[:, z], shared_out.at[here.z], here.line(z)) for z in here.on_line()
    ]
    for job in jobs:
        job.second()
    for job in jobs:
        job.third()
    for job in jobs:
        job.finish()
    for copy in moved:
        copy.wait_recv()
    kept.wait()
    mine.wait()
    wire.close()


def fan_plane(block, shared):
    out, shared = call(
        fan_kernel,
        5,
        [((PLANE,) + block.shape, block.dtype), ((LINE, PLANE) + shared.shape[2:], BF16)],
        [block, shared],
        wires(2 * PLANE_GATHER_COPIES + 3) + [pltpu.SemaphoreType.DMA((2,))],
        in_specs=[VMEM, HBM],
    )
    return out.reshape(PLANE * block.shape[0], block.shape[1]), shared


def end_kernel(
    parts, ffn, three, output, shared, bias, terms,
    out, ffn_out, three_out, output_out, shared_out, bias_out, terms_out,
    send, recv, local, held, ffn_held, three_held, output_held, *rooms
):
    here, wire = Place(), Wire(send, recv)
    room, ffn_rooms = rooms[:5], [rooms[5 + 5 * i : 10 + 5 * i] for i in range(4)]
    ffn_room, three_room, output_room = rooms[25:27], rooms[27:29], rooms[29:31]
    terms_in, terms_own, terms_line = rooms[31:]
    others = [(here.c + step) % PLANE for step in range(1, PLANE)]
    greet([here.plane(c) for c in others] + [here.line(z) for z in here.on_line()])
    on_line = here.on_line()
    places = [here.mirrored(i) for i in (2, 3, 1, 0)]
    loads = [
        pltpu.make_async_copy(three.at[:, z], three_held.at[z], local.at[z]) for z in range(LINE)
    ]
    loads += [
        pltpu.make_async_copy(parts, held, local.at[4]),
        pltpu.make_async_copy(output, output_held, local.at[5]),
        pltpu.make_async_copy(terms.at[here.c], terms_own, local.at[6]),
        pltpu.make_async_copy(bias, bias_out.at[here.z], local.at[7]),
    ]
    shared_own = pltpu.make_async_copy(shared.at[:, here.c], shared_out.at[here.c], local.at[8])
    shared_own.start()
    loads += [
        pltpu.make_async_copy(ffn.at[z], ffn_held.at[i], local.at[9 + i])
        for i, z in enumerate(places)
    ]
    for copy in loads:
        copy.start()
    job = PlaneScatter(wire, here, held, room)
    ffn_jobs = [PlaneScatter(wire, here, ffn_held.at[i], ffn_rooms[i]) for i in range(4)]
    three_line = LineScatter(
        wire, here, [three_held.at[here.mirrored(i)] for i in range(4)], three_room
    )
    output_line = LineScatter(
        wire, here, [output_held.at[here.mirrored(i)] for i in range(4)], output_room
    )
    ffn_line = LineScatter(wire, here, [ffn_jobs[i].mine() for i in (3, 2, 0, 1)], ffn_room)
    for copy in loads[:4]:
        copy.wait()
    three_line.begin()
    loads[4].wait()
    job.begin()
    for copy in loads[5:]:
        copy.wait()
    terms_plane = [
        wire.push(terms.at[c], terms_in.at[j], here.plane(c)) for j, c in enumerate(others)
    ]
    shared_plane = [
        wire.push(shared.at[:, c], shared_out.at[here.c], here.plane(c)) for c in others
    ]
    bias_line = [wire.push(bias, bias_out.at[here.z], here.line(z)) for z in on_line]
    ffn_jobs[0].begin()
    ffn_jobs[1].begin()
    job.first()
    output_line.begin()
    ffn_jobs[0].first()
    job.second()
    ffn_jobs[2].begin()
    ffn_jobs[1].first()
    ffn_jobs[0].second()
    for copy in terms_plane:
        copy.wait_recv()
    total = terms_own[...]
    for j in range(PLANE - 1):
        total += terms_in[j]
    terms_own[...] = total
    terms_last = [
        wire.push(terms_own.at[z], terms_line.at[j], here.line(z)) for j, z in enumerate(on_line)
    ]
    three_line.first()
    job.third()
    out[...] = job.mine()[...].astype(F32)
    ffn_jobs[3].begin()
    ffn_jobs[2].first()
    ffn_jobs[1].second()
    ffn_jobs[0].third()
    ffn_jobs[3].first()
    ffn_jobs[2].second()
    ffn_jobs[1].third()
    three_line.second()
    ffn_jobs[3].second()
    ffn_jobs[2].third()
    ffn_line.begin()
    output_line.first()
    ffn_jobs[3].third()
    three_line.third()
    three_plane = [
        wire.push(three_held.at[here.z, c], three_out.at[here.c], here.plane(c)) for c in others
    ]
    kept = pltpu.make_async_copy(three_held.at[here.z, here.c], three_out.at[here.c], local.at[0])
    kept.start()
    ffn_line.first()
    output_line.second()
    ffn_line.second()
    output_line.third()
    output_out[...] = output_held[here.z].astype(F32)
    for copy in terms_last:
        copy.wait_recv()
    terms_out[...] = terms_own[here.z] + terms_line[0] + terms_line[1] + terms_line[2]
    ffn_line.third()
    ffn_out[...] = ffn_held[3 - here.depth, here.y * 2 + here.x, here.core].astype(F32)
    for copy in bias_line + shared_plane + three_plane:
        copy.wait_recv()
    kept.wait()
    shared_own.wait()
    wire.close()


def line_room(shape, kind):
    return [pltpu.VMEM((3,) + shape, kind), pltpu.VMEM((2,) + shape, kind)]


def end_transfers(parts, ffn, three, output, shared, bias, terms):
    rows, width = parts.shape[0] // PLANE, parts.shape[1]
    _, _, owned, wide = three.shape
    copies = 5 * PLANE_SCATTER_COPIES + 3 * LINE_SCATTER_COPIES + 3 + 7 + 3 + 7 + 7
    return call(
        end_kernel,
        6,
        [
            ((rows, width), F32),
            ((rows, width), F32),
            ((PLANE, owned, wide), BF16),
            ((owned, width), F32),
            ((PLANE, LINE) + shared.shape[2:], BF16),
            ((LINE,) + bias.shape, F32),
            (terms.shape[2:], F32),
        ],
        [parts.reshape(4, 2, rows, width), ffn, three, output, shared, bias, terms],
        wires(copies)
        + [
            pltpu.SemaphoreType.DMA((13,)),
            pltpu.VMEM((4, 2, rows, width), BF16),
            pltpu.VMEM((LINE, 4, 2, rows, width), BF16),
            pltpu.VMEM((LINE, PLANE, owned, wide), BF16),
            pltpu.VMEM((LINE, owned, width), BF16),
        ]
        + scatter_room(rows, width, BF16) * 5
        + line_room((rows, width), BF16)
        + line_room((PLANE, owned, wide), BF16)
        + line_room((owned, width), BF16)
        + [
            pltpu.VMEM((PLANE - 1,) + terms.shape[1:], F32),
            pltpu.VMEM(terms.shape[1:], F32),
            pltpu.VMEM((3,) + terms.shape[2:], F32),
        ],
        out_specs=[VMEM, VMEM, HBM, VMEM, HBM, HBM, VMEM],
        in_specs=[HBM] * 5 + [VMEM, HBM],
    )


def rms_scale(values):
    return lax.rsqrt(jnp.mean(values * values, axis=-1, keepdims=True) + EPS)


def rope_tables(places, head_size):
    half = head_size // 2
    freqs = jnp.exp(jnp.arange(half, dtype=F32) * (-2.0 * math.log(ROPE_BASE) / head_size))
    angles = places.astype(F32)[:, None] * freqs[None, :]
    return (jnp.cos(angles)[:, None, :], jnp.sin(angles)[:, None, :])


def rotate(values, cosine, sine):
    half = values.shape[-1] // 2
    first = values[..., :half]
    second = values[..., half:]
    return jnp.concatenate(
        [first * cosine - second * sine, second * cosine + first * sine], axis=-1
    )


def dot(left, right):
    return jnp.dot(left, right, preferred_element_type=F32)


def times_back(left, right):
    return lax.dot_general(left, right, (((1,), (1,)), ((), ())), preferred_element_type=F32)


def outer_sum(left, right):
    return lax.dot_general(left, right, (((0,), (0,)), ((), ())), preferred_element_type=F32)


def gather_plane(shard):
    return lax.all_gather(shard, "ctx", axis=0, tiled=True)


def scatter_plane(partial):
    return lax.psum_scatter(partial, "ctx", scatter_dimension=0, tiled=True)


def scatter_line(partial):
    return lax.psum_scatter(partial, "fsdp", scatter_dimension=0, tiled=False)


def over(step, carry, items, unrolled):
    if not unrolled:
        return lax.scan(step, carry, items)
    outs = []
    for i in range(jax.tree.leaves(items)[0].shape[0]):
        carry, out = step(carry, jax.tree.map(lambda item: item[i], items))
        outs.append(out)
    return carry, jax.tree.map(lambda *parts: jnp.stack(parts), *outs)


def blocks(length):
    return length // min(length, BLOCK)


def cut(array, axis=0):
    shape = array.shape
    count = blocks(shape[axis])
    shape = shape[:axis] + (count, shape[axis] // count) + shape[axis + 1 :]
    return jnp.moveaxis(array.reshape(shape), axis, 0)


def attend(queries, keys, values, starts):
    length = queries.shape[0]
    scale = 1.0 / math.sqrt(HEAD)
    cols = jnp.arange(length, dtype=jnp.int32)[None, :]

    def step(carry, items):
        part, low, rows = items
        mask = ((cols <= rows[:, None]) & (cols >= low[:, None]))[None]
        scores = jnp.einsum("qhd,khd->hqk", part, keys, preferred_element_type=F32)
        scores = jnp.where(mask, scores * scale, MASKED)
        best = jnp.max(scores, axis=-1, keepdims=True)
        weights = jnp.exp(scores - best)
        total = jnp.sum(weights, axis=-1, keepdims=True)
        probs = (weights / total).astype(BF16)
        out = jnp.einsum("hqk,khd->qhd", probs, values, preferred_element_type=F32)
        return carry, (out, best + jnp.log(total))

    items = (cut(queries), cut(starts), cut(cols[0]))
    _, (outs, logs) = over(step, 0, items, blocks(length) == 1)
    return outs.reshape(queries.shape), jnp.moveaxis(logs, 0, 1).reshape(-1, length, 1)


def attend_back(queries, keys, values, starts, logs, grad_attn, delta):
    length = queries.shape[0]
    scale = 1.0 / math.sqrt(HEAD)
    cols = jnp.arange(length, dtype=jnp.int32)[None, :]

    def step(carry, items):
        grad_keys, grad_values = carry
        part, low, rows, log, grad, less = items
        mask = ((cols <= rows[:, None]) & (cols >= low[:, None]))[None]
        scores = jnp.einsum("qhd,khd->hqk", part, keys, preferred_element_type=F32)
        probs = jnp.where(mask, jnp.exp(scores * scale - log), 0.0)
        grad_probs = jnp.einsum("qhd,khd->hqk", grad, values, preferred_element_type=F32)
        grad_scores = (probs * (grad_probs - less[:, :, None])).astype(BF16)
        grad_queries = scale * jnp.einsum(
            "hqk,khd->qhd", grad_scores, keys, preferred_element_type=F32
        )
        grad_keys += scale * jnp.einsum(
            "hqk,qhd->khd", grad_scores, part, preferred_element_type=F32
        )
        grad_values += jnp.einsum(
            "hqk,qhd->khd", probs.astype(BF16), grad, preferred_element_type=F32
        )
        return (grad_keys, grad_values), grad_queries

    zeros = jnp.zeros(keys.shape, F32)
    items = (cut(queries), cut(starts), cut(cols[0]), cut(logs, 1), cut(grad_attn), cut(delta, 1))
    carry, grad_queries = over(step, (zeros, zeros), items, blocks(length) == 1)
    return grad_queries.reshape(queries.shape), carry[0], carry[1]


def body(
    tokens,
    positions,
    routes,
    cotangent,
    attn_gain,
    query_weight,
    key_weight,
    value_weight,
    query_bias,
    key_bias,
    value_bias,
    output_weight,
    ffn_gain,
    router_weight,
    expert_gate,
    expert_up,
    expert_down,
    shared_gate,
    shared_up,
    shared_down,
    shared_sigmoid,
):
    plane, line = lax.axis_size("ctx"), lax.axis_size("fsdp")
    place = lax.axis_index("ctx")
    rows, width = tokens.shape[1], tokens.shape[2]
    length = plane * rows
    experts = router_weight.shape[1]
    groups = math.gcd(HEADS, plane)
    share = plane // groups
    heads = HEADS // groups
    span = heads * HEAD
    owned = width // (plane * line)
    group = place // share

    fast = (plane, line) == (PLANE, LINE) and share == 1
    three = jnp.stack([query_weight, key_weight, value_weight])
    routed_units, shared_units = expert_down.shape[1], shared_down.shape[0]
    columns = [attn_gain, query_bias, key_bias, value_bias, ffn_gain, shared_sigmoid]
    columns = jnp.concatenate([jnp.stack(columns, axis=1), router_weight], axis=1)
    x_own, g_own = tokens[0], cotangent[0]
    shared = [w.reshape(owned, plane * line, shared_units) for w in (shared_gate, shared_up)]
    shared = jnp.concatenate(shared, axis=2).transpose(1, 0, 2)
    routed = jnp.stack([expert_gate[0].T, expert_up[0].T]).reshape(2, line, routed_units, -1)
    routed = routed.transpose(1, 0, 2, 3)
    if fast:
        high, low = positions[0] // 64, positions[0] % 64
        digits = jnp.stack([high, low]).reshape(2 * (rows // owned), owned).T.astype(BF16)
        small = jnp.concatenate([columns, digits], axis=1)
        marks = small.shape[1]
        small = jnp.pad(small, ((0, 0), (0, LANES - marks)))
        sent = three.reshape(3, owned, plane, span).transpose(2, 1, 0, 3)
        x_all, w_three, w_output, small, shared, g_sent = start_transfers(
            x_own,
            sent.reshape(plane, owned, 3 * span),
            output_weight,
            small,
            shared.reshape(plane, line, owned, 2 * shared_units),
            g_own,
        )
        routed = routed.reshape(line, 2 * routed_units, -1)
        routed = lax.all_to_all(routed, "fsdp", split_axis=0, concat_axis=0, tiled=True)
        x_all = x_all.reshape(length, width)
        w_three = w_three.reshape(width, 3 * span)
        w_output = w_output.reshape(span, width)
        digits = lax.dynamic_index_in_dim(small, lax.axis_index("fsdp"), 1, keepdims=False)
        digits = digits[:, :, columns.shape[1] : marks].astype(jnp.int32)
        digits = digits.transpose(0, 2, 1).reshape(plane, 2, rows)
        places = (digits[:, 0] * 64 + digits[:, 1]).reshape(length)
        small = small.reshape(width, LANES)[:, : columns.shape[1]]
        g_all = lax.all_gather(g_sent, ("fsdp", "ctx"), axis=0, tiled=True)
    else:
        small = lax.all_gather(columns, BOTH, axis=0, tiled=True)
        places = lax.all_gather(positions[0], "ctx", axis=0, tiled=True)
        x_all = gather_plane(x_own)
        whole = lax.all_gather(three, BOTH, axis=1, tiled=True)
        whole = lax.dynamic_slice_in_dim(whole, group * span, span, 2)
        w_three = whole.transpose(1, 0, 2).reshape(width, 3 * span)
        w_output = lax.all_gather(output_weight, BOTH, axis=0, tiled=True)
        w_output = lax.dynamic_slice_in_dim(w_output, group * span, span, 0)
    gain_in = small[:, 0].astype(F32)
    gain_mid = small[:, 4].astype(F32)
    w_switch = small[:, 5]
    w_router = small[:, 6:]
    biases = lax.dynamic_slice_in_dim(small[:, 1:4], group * span, span, 0).astype(F32)
    biases = biases.T.reshape(3 * span)
    used = routed_units + shared_units
    units = -(-used // LANES) * LANES

    states = x_all.astype(F32)
    starts = jnp.arange(length, dtype=jnp.int32) - places
    unit_in = states * rms_scale(states)
    normed = (unit_in * gain_in[None, :]).astype(BF16)
    cosine, sine = rope_tables(places, HEAD)
    pre = (dot(normed, w_three) + biases[None, :]).reshape(length, 3, heads, HEAD)
    queries = rotate(pre[:, 0], cosine, sine).astype(BF16)
    keys = rotate(pre[:, 1], cosine, sine).astype(BF16)
    values = pre[:, 2].astype(BF16)
    attn_rows, logs = attend(queries, keys, values, starts)
    if share > 1:
        mine = jnp.arange(length, dtype=jnp.int32) // (length // share) == place % share
        attn_rows = jnp.where(mine[:, None, None], attn_rows, 0.0)
    attn_low = attn_rows.reshape(length, span).astype(BF16)
    branch = dot(attn_low, w_output).astype(BF16)
    if fast:
        branch, shared = fold_plane(branch, shared)
    else:
        branch = scatter_plane(branch).astype(F32)
    mid = x_own.astype(F32) + branch

    scale_mid = rms_scale(mid)
    unit_mid = mid * scale_mid
    normed2 = (unit_mid * gain_mid[None, :]).astype(BF16)
    router_probs = jax.nn.softmax(dot(normed2, w_router), axis=-1)
    picks = routes[0][:, :, None] == jnp.arange(experts, dtype=jnp.int32)[None, None, :]
    hits = jnp.any(picks, axis=1)
    switch = jax.nn.sigmoid(dot(normed2, w_switch[:, None]))
    factors = jnp.concatenate([jnp.where(hits, router_probs, 0.0), switch], axis=1)
    mine = jnp.arange(experts, dtype=jnp.int32) == place

    def hidden_units(x_all, g_all, by_route, by_switch, w_both, w_down):
        number = jnp.arange(units, dtype=jnp.int32)
        by = jnp.where(number < routed_units, by_route[:, None], by_switch[:, None])
        pre = times_back(x_all, w_both)
        gate_pre, up_pre = pre[:, :units], pre[:, units:]
        grad_hidden = times_back(g_all, w_down)
        sigma = jax.nn.sigmoid(gate_pre)
        act = gate_pre * sigma
        hidden = act * up_pre
        product = hidden * grad_hidden
        routed_dot = jnp.sum(product[:, :routed_units], axis=1)
        shared_dot = jnp.sum(product[:, routed_units:used], axis=1)
        weighted = (hidden * by).astype(BF16)
        slope = sigma * (1.0 + gate_pre * (1.0 - sigma))
        grad_hidden = grad_hidden * by
        grad_pre = jnp.concatenate([grad_hidden * up_pre * slope, grad_hidden * act], axis=1)
        grad_pre = grad_pre.astype(BF16)
        grad_part = dot(grad_pre, w_both).astype(BF16)
        out_part = dot(weighted, w_down).astype(BF16)
        terms = (outer_sum(grad_pre, x_all), outer_sum(weighted, g_all))
        return terms, out_part, grad_part, routed_dot, shared_dot

    def units_of(routed, shared, spare):
        return jnp.concatenate([routed[0], shared[0], spare, routed[1], shared[1], spare], axis=0)

    def parts_of(term):
        routed = [term[:routed_units], term[units : units + routed_units]]
        shared = [term[routed_units:used], term[units + routed_units : units + used]]
        return jnp.stack(routed), jnp.stack(shared)

    if fast:
        few = jnp.pad(factors.T, ((0, 16 - experts - 1), (0, 0)))
        shared = shared.reshape(width, 2 * shared_units).T
        x_all, grad_ffn, dots, out_part, grad_pre, weighted = feed_forward(
            normed2, few, g_all, routed, shared, expert_down[0], shared_down, units
        )
        term_both = outer_sum(
            grad_pre.reshape(line * length, 2 * units), x_all.reshape(line * length, width)
        )
        term_down = outer_sum(weighted.reshape(line * length, units), g_all)
        routed, shared = parts_of(term_both.astype(BF16))
        routed = routed.reshape(2 * routed_units, line, -1).transpose(1, 0, 2)
        routed = lax.all_to_all(routed, "fsdp", split_axis=0, concat_axis=0, tiled=True)
        routed = routed.reshape(line, 2, routed_units, -1)
        shared = shared.reshape(2 * shared_units, width).T
        shared = shared.reshape(plane, line, owned, 2 * shared_units)
        dots = dots[: experts + 1].T
    else:
        routed = lax.all_to_all(routed, "fsdp", split_axis=0, concat_axis=0, tiled=True)
        routed = routed.transpose(1, 2, 0, 3).reshape(2, routed_units, width)
        spare = jnp.zeros((units - used, width), BF16)
        w_down = jnp.concatenate([expert_down[0], shared_down, spare], axis=0)
        factors = lax.all_gather(factors, ("fsdp", "ctx"), axis=0, tiled=True)
        factors = factors.reshape(line, length, experts + 1)
        x_line = lax.all_gather(normed2, "fsdp", axis=0, tiled=False)
        g_line = lax.all_gather(g_own, "fsdp", axis=0, tiled=False)

        shared = lax.all_to_all(shared, BOTH, split_axis=0, concat_axis=0, tiled=True)
        shared = shared.reshape(width, 2, shared_units).transpose(1, 2, 0)
        w_both = units_of(routed, shared, spare)

        def step(terms, items):
            x_part, g_part, factor = items
            by_route = jnp.sum(jnp.where(mine, factor[:, :experts], 0.0), axis=1)
            more, out_part, grad_part, routed_dot, shared_dot = hidden_units(
                gather_plane(x_part), gather_plane(g_part), by_route, factor[:, experts], w_both, w_down
            )
            dots = jnp.where(mine, routed_dot[:, None], 0.0)
            dots = jnp.concatenate([dots, shared_dot[:, None]], axis=1)
            terms = tuple(term + part for term, part in zip(terms, more))
            return terms, (scatter_plane(out_part), scatter_plane(grad_part), dots)

        terms = tuple(jnp.zeros(w.shape, F32) for w in (w_both, w_down))
        terms, (out_parts, grad_parts, dots) = lax.scan(step, terms, (x_line, g_line, factors))
        term_both, term_down = terms
        grad_ffn = scatter_line(grad_parts).astype(F32)
        ffn = scatter_line(out_parts).astype(F32)
        dots = dots.reshape(line, plane, rows, experts + 1)
        dots = lax.psum_scatter(dots, "ctx", scatter_dimension=1, tiled=False)
        dots = scatter_line(dots)

        routed, shared = parts_of(term_both.astype(BF16))
        grad_shared_gate, grad_shared_up = [
            lax.all_to_all(t.T, BOTH, split_axis=0, concat_axis=1, tiled=True).astype(F32)
            for t in shared
        ]
        routed = routed.reshape(2, routed_units, line, -1).transpose(2, 0, 1, 3)
        routed = lax.all_to_all(routed, "fsdp", split_axis=0, concat_axis=0, tiled=True)
    grad_expert_down = term_down[:routed_units][None]
    grad_shared_down = term_down[routed_units:used]

    grad_out = cotangent[0].astype(F32)
    grad_probs = jnp.where(hits, dots[:, :experts], 0.0)
    grad_logits = (
        router_probs * (grad_probs - jnp.sum(router_probs * grad_probs, axis=-1, keepdims=True))
    ).astype(BF16)
    grad_switch = dots[:, experts:] * switch * (1.0 - switch)
    grad_normed2 = (
        grad_ffn + times_back(grad_logits, w_router) + grad_switch * w_switch.astype(F32)[None, :]
    )
    scaled_mid = grad_normed2 * gain_mid[None, :]
    grad_mid = grad_out + scale_mid * (
        scaled_mid - unit_mid * jnp.mean(scaled_mid * unit_mid, axis=-1, keepdims=True)
    )
    terms = jnp.concatenate(
        [
            jnp.sum(grad_normed2 * unit_mid, axis=0)[:, None],
            jnp.sum(grad_switch * normed2.astype(F32), axis=0)[:, None],
            outer_sum(normed2, grad_logits),
        ],
        axis=1,
    )

    grad_branch = grad_mid.astype(BF16)
    if fast:
        grad_branch, shared = fan_plane(grad_branch, shared)
    else:
        grad_branch = gather_plane(grad_branch)
    routed = routed.transpose(1, 3, 0, 2).reshape(2, 1, -1, line * routed_units).astype(F32)
    grad_attn = times_back(grad_branch, w_output).reshape(length, heads, HEAD).astype(BF16)
    if share > 1:
        mine = jnp.arange(length, dtype=jnp.int32) // (length // share) == place % share
        grad_attn = jnp.where(mine[:, None, None], grad_attn, 0)
    delta = jnp.sum(grad_attn.astype(F32) * attn_rows, axis=-1).T
    grad_queries, grad_keys, grad_values = attend_back(
        queries, keys, values, starts, logs, grad_attn, delta
    )
    grad_pre = jnp.concatenate(
        [
            rotate(grad_queries, cosine, -sine).reshape(length, span),
            rotate(grad_keys, cosine, -sine).reshape(length, span),
            grad_values.reshape(length, span),
        ],
        axis=1,
    ).astype(BF16)
    grad_part = times_back(grad_pre, w_three).astype(BF16)
    term_three = outer_sum(normed, grad_pre)
    term_output = outer_sum(attn_low, grad_branch)
    term_bias = jnp.sum(grad_pre.astype(F32), axis=0)
    if fast:
        count = terms.shape[1]
        terms = terms.reshape(plane, line, owned * count)
        terms = jnp.pad(terms, ((0, 0), (0, 0), (0, 8 * LANES - owned * count)))
        grad_normed, ffn, grad_three, grad_output, shared, term_bias, terms = end_transfers(
            grad_part,
            out_part,
            term_three.astype(BF16).reshape(plane, line, owned, 3 * span),
            term_output.astype(BF16).reshape(line, owned, width),
            shared,
            jnp.broadcast_to(term_bias[None], (8, 3 * span)),
            terms.reshape(plane, line, 8, LANES),
        )
        grad_three = grad_three.reshape(plane, owned, 3, span).transpose(2, 1, 0, 3)
        grad_three = grad_three.reshape(3, owned, width).astype(F32)
        term_bias = jnp.sum(term_bias[:, 0], axis=0).reshape(3, line, owned)
        grad_bias = lax.dynamic_index_in_dim(term_bias, lax.axis_index("fsdp"), 1, keepdims=False)
        terms = terms.reshape(-1)[: owned * count].reshape(owned, count)
        shared = shared.reshape(plane * line, owned, 2, shared_units).transpose(2, 1, 0, 3)
        shared = shared.reshape(2, owned, -1).astype(F32)
        grad_shared_gate, grad_shared_up = shared[0], shared[1]
    else:
        grad_normed = scatter_plane(grad_part).astype(F32)
        zeros = jnp.zeros((3, width, width), BF16)
        spread = lax.dynamic_update_slice_in_dim(
            zeros, term_three.astype(BF16).reshape(width, 3, span).transpose(1, 0, 2), group * span, 2
        )
        grad_three = lax.psum_scatter(spread, BOTH, scatter_dimension=1, tiled=True).astype(F32)
        spread = lax.dynamic_update_slice_in_dim(
            zeros[0], term_output.astype(BF16), group * span, 0
        )
        grad_output = lax.psum_scatter(spread, BOTH, scatter_dimension=0, tiled=True).astype(F32)
        spread = lax.dynamic_update_slice_in_dim(
            jnp.zeros((3, width), F32), term_bias.reshape(3, span), group * span, 1
        )
        grad_bias = lax.psum_scatter(spread, BOTH, scatter_dimension=1, tiled=True)
        terms = lax.psum_scatter(terms, BOTH, scatter_dimension=0, tiled=True)
    grad_attn_gain = jnp.sum(three.astype(F32) * grad_three, axis=(0, 2)) / attn_gain.astype(F32)
    own_states = tokens[0].astype(F32)
    scale_in = rms_scale(own_states)
    own_unit = own_states * scale_in
    scaled_in = grad_normed * gain_in[None, :]
    grad_states = grad_mid + scale_in * (
        scaled_in - own_unit * jnp.mean(scaled_in * own_unit, axis=-1, keepdims=True)
    )
    return (
        (mid + ffn).astype(BF16)[None],
        grad_states[None],
        grad_attn_gain,
        grad_three[0],
        grad_three[1],
        grad_three[2],
        grad_bias[0],
        grad_bias[1],
        grad_bias[2],
        grad_output,
        terms[:, 0],
        terms[:, 2:],
        routed[0],
        routed[1],
        grad_expert_down,
        grad_shared_gate,
        grad_shared_up,
        grad_shared_down,
        terms[:, 1],
    )


def solution(mesh):
    tokens, flat, both, routed = (
        P("fsdp", "ctx", None),
        P(BOTH),
        P(BOTH, None),
        P("ctx", "fsdp", None),
    )
    weights = (flat, both, both, both, flat, flat, flat, both, flat, both)
    weights += (routed, routed, routed, both, both, both, flat)
    return jax.shard_map(
        body,
        mesh=mesh,
        in_specs=(tokens, P("fsdp", "ctx"), tokens, tokens) + weights,
        out_specs=(tokens, tokens) + weights,
        check_vma=False,
    )
```

time: 5980 us -> 916 us (0.15)
  waiting for transfers between devices: 4940 us -> 36.9 us
  Pallas kernels: 0 us -> 606 us
  matrix products: 386 us -> 95 us
  starting transfers between devices: 275 us -> 9.76 us
  blocking collectives: 231 us -> 0 us
    reduce_scatter x10 -> x0, waiting for transfers between devices: 4350 us -> none  [the longest x1 976 us: body(): lax.psum_scatter(term_shared_down, ('ctx', 'fsdp'), scatter_dimension=0,...]
    pallas_call x0 -> x5, Pallas kernels: none -> 606 us  [call(): pl.pallas_call(kernel, out_shape=[jax.ShapeDtypeStruct(shape, kind) for s...]
    all_gather x10 -> x1, waiting for transfers between devices: 498 us -> 27.1 us  [body(): g_all = lax.all_gather(g_sent, ('fsdp', 'ctx'), axis=0, tiled=True)]
    dot_general x94 -> x18, matrix products: 385 us -> 95 us  [the longest x5 51.3 us: outer_sum(): lax.dot_general(left, right, (((0,), (0,)), ((), ())), preferred_element_...]
    ppermute x46 -> x0, starting transfers between devices: 247 us -> none  [the longest x30 185 us: from_behind(): lax.ppermute(value, axis, [(source, source + steps) for source in range(l...]
    unnamed x2 -> x0, blocking collectives: 88.7 us -> none
    all_to_all x3 -> x2, waiting for transfers between devices: 87.7 us -> 9.8 us  [body(): lax.all_to_all(routed, 'fsdp', split_axis=0, concat_axis=0, tiled=True)]
    all_to_all x1 -> x0, blocking collectives: 74.5 us -> none  [body(): lax.all_to_all(to_owners(expert_out, cycle_size, local_experts, capacity,...]
  transfers between devices with their start and end apart: 70 -> 3, of which waited for: 18 -> 2; matrix products, arithmetic and copies ran while one was open for 8% -> 11% of each run, Pallas kernels for 0% -> 12%
where the time goes in v1:
time: 916 us; the launch traced here: 908 us
  Pallas kernels  606 us (66%)
  local copies, waits for them, and re-layouts  108 us (12%)
  matrix products  95 us (10%)
  other arithmetic  37.1 us (4%)
  waiting for transfers between devices  36.9 us (4%)
  between operations  15.2 us (2%)
  starting transfers between devices  9.76 us (1%)
    pallas_call x5, Pallas kernels, call(): pl.pallas_call(kernel, out_shape=[jax.ShapeDtypeStruct(shape, kind) for s...  606 us
    dot_general x5, matrix products, outer_sum(): lax.dot_general(left, right, (((0,), (0,)), ((), ())), preferred_element_...  51.3 us
    all_gather x1, waiting for transfers between devices, body(): g_all = lax.all_gather(g_sent, ('fsdp', 'ctx'), axis=0, tiled=True)  27.1 us
    unnamed x124, local copies, waits for them, and re-layouts  26.3 us
  transfers between devices with their start and end apart: 3, of which 2 were waited for; matrix products, arithmetic and copies ran while one was open for 11% of the time, Pallas kernels for 12%

profile of v1, /device:TPU:0, one launch (start us, length us, event | category | flops | bytes accessed | tf_op | source)
XLA Modules:
  0.0 908.0 jit_solution(10235300949615092000)
XLA Ops:
  14.2 2.0 reshape.445
  16.9 3.0 reshape.444
  23.8 99.9 %shard_map.348 = (bf16[8,128,2048]{2,1,0:T(8,128)(2,1)}, bf16[8,4,64,768]{3,2,1,0:T(8,128)(2,1)}, bf16[4,64,2048]{2,1,0:T(8,128)(2,1)}, bf16[8,4,64,128]{3,2,1,0...) custom-call(bf16[128,2048]{1,0:T(8,128)(2,1)} %bitcast.225, ...), custom_call_target="tpu_custom_call", output_to_operand_aliasing={{5}: (5, {})} | custom-call | tf_op jit(solution)/shard_map/pallas_call | solution.py:332
  128.2 4.9 all-to-all-start
  135.6 3.2 multiply_reduce_fusion
  140.9 3.6 convolution_add_fusion.1
  150.0 3.0 fusion.36
  154.4 2.3 select_reduce_fusion
  156.7 2.2 fusion.2
  160.0 5.1 fusion.61
  165.1 3.3 convolution_convert_fusion
  168.4 107.5 %shard_map.349 = (f32[128,2048]{1,0:T(8,128)}, bf16[8,4,64,352]{3,2,1,0:T(8,128)(2,1)}) custom-call(bf16[4,2,128,2048]{3,2,1,0:T(8,128)(2,1)} %bitcast.216, bf16[4,8,64,352]{3,2,1,0:T(8,128)(2,1)} %get-tuple-element.46.shared), custom_call_target="tpu_custom_call" | custom-call | tf_op jit(solution)/shard_map/pallas_call | solution.py:332
  275.9 2.5 copy.223
  282.2 3.0 fusion.1
  285.2 27.1 %all-gather.2.cloned.1.call-done = bf16[4096,2048]{1,0:T(8,128)(2,1)} async-done(((bf16[128,2048]{1,0:T(8,128)(2,1)}), bf16[4096,2048]{1,0:T(8,128)(2,1)}) %all-gather.2.cloned.1.call-update) | async-done | bytes 16777232 | tf_op jit(solution)/shard_map/all_gather | solution.py:1156
  312.2 204.0 %shard_map.350 = (bf16[4,8,128,2048]{3,2,1,0:T(8,128)(2,1)}, f32[128,2048]{1,0:T(8,128)}, f32[16,128]{1,0:T(8,128)}, bf16[4,4,2,128,2048]{4,3,2,1,0:T(8,128)(2,1...) custom-call(bf16[128,2048]{1,0:T(8,128)(2,1)} %copy-done.3, f32[16,128]{1,0:T(8,128)} %pad.13.few, ...), custom_call_target="tpu_custom_call" | custom-call | tf_op jit(solution)/shard_map/pallas_call | solution.py:332
  518.9 27.9 %bitcast_convert_fusion = bf16[1280,2048]{1,0:T(8,128)(2,1)S(1)} fusion(bf16[4,8,128,1280]{3,2,1,0:T(8,128)(2,1)} %get-tuple-element.52, bf16[4,8,128,2048]{3,2,1,0:T(8,128)(2,1)} %get-tuple-element.53), kind=kOutput, calls=%fused_computation | convolution fusion | flops 21477457920 | bytes 32505856 | tf_op jit(solution)/shard_map/dot_general | solution.py:998
  546.8 2.3 copy-done.17
  550.5 2.7 copy.225
  554.3 31.5 %shard_map.351 = (bf16[8,128,2048]{2,1,0:T(8,128)(2,1)}, bf16[4,8,64,352]{3,2,1,0:T(8,128)(2,1)}) custom-call(bf16[128,2048]{1,0:T(8,128)(2,1)} %fusion.56.block, bf16[8,4,64,352]{3,2,1,0:T(8,128)(2,1)} %bitcast.229), custom_call_target="tpu_custom_call" | custom-call | tf_op jit(solution)/shard_map/pallas_call | solution.py:332
  585.8 4.2 multiply_reduce_fusion.4
  590.1 6.6 fusion.13
  596.7 4.4 multiply_convert_fusion
  601.2 2.0 fusion.12
  608.1 2.0 copy.232
  610.2 7.8 convolution_convert_fusion.1
  618.7 4.1 slice_bitcast_fusion.2
  622.8 5.3 convolution_convert_fusion.2
  628.1 2.3 convolution_convert_fusion.3
  634.9 163.2 %shard_map.352 = (f32[128,2048]{1,0:T(8,128)}, f32[128,2048]{1,0:T(8,128)}, bf16[8,64,768]{2,1,0:T(8,128)(2,1)}, f32[64,2048]{1,0:T(8,128)}, bf16[8,4,64,352]{3,...) custom-call(bf16[4,2,128,2048]{3,2,1,0:T(8,128)(2,1)} %bitcast.237, ...), custom_call_target="tpu_custom_call" | custom-call | tf_op jit(solution)/shard_map/pallas_call | solution.py:332
  798.1 3.6 reshape.480
  801.6 3.1 multiply_reduce_fusion.1
  809.6 3.6 pad_maximum_fusion
  813.2 7.1 reshape.471
  820.3 4.0 copy.279
  824.3 4.8 all-to-all-start.1
  829.0 6.2 reshape.482
  835.2 9.1 %fusion.58 = (f32[1,64,32,176]{3,0,1,2:T(1,128)}, f32[1,64,32,176]{3,0,1,2:T(1,128)S(1)}) fusion(f32[2,64,32,176]{3,0,1,2:T(2,128)} %bitcast.218), kind=kLoop, calls=%fused_computation.157 | loop fusion | bytes 5767168 | tf_op jit(solution)/shard_map/slice | solution.py:1365
  844.4 2.5 copy.241
  846.9 3.3 squeeze.91
  850.2 4.1 copy.242
  854.3 3.3 squeeze.92
  857.6 15.7 %fusion.64 = f32[640,2048]{1,0:T(8,128)S(1)} fusion(bf16[4096,640]{1,0:T(8,128)(2,1)} %bitcast.294, bf16[4096,2048]{1,0:T(8,128)(2,1)} %all-gather.2.cloned.1.call-done), kind=kOutput, calls=%fused_computation.163 | convolution fusion | flops 10737418240 | bytes 27262976 | tf_op jit(solution)/shard_map/dot_general | solution.py:998
  879.9 9.8 %all-to-all-done.1 = bf16[4,704,512]{2,1,0:T(8,128)(2,1)} async-done(((bf16[4,704,512]{2,1,0:T(8,128)(2,1)}), bf16[4,704,512]{2,1,0:T(8,128)(2,1)}, u32[]{:S(2)}, u32[]{:S(2)}) %all-to-all-start.1) | async-done | bytes 2883616 | tf_op jit(solution)/shard_map/all_to_all | solution.py:1248
  889.7 2.6 convert_bitcast_fusion
  892.3 2.2 fusion.57
  894.6 3.4 copy.244
  897.9 2.2 copy.245
  (204 shorter events, 59.2 us)
Async XLA Ops:
  7.2 6.6 copy-start.49
  7.2 6.7 copy-start.45
  7.2 6.7 copy-start.40
  7.2 6.6 copy-start.41
  7.2 6.6 copy-start.42
  7.2 6.6 copy-start.43
  7.3 6.6 copy-start.44
  7.3 6.6 copy-start.39
  7.3 7.0 copy-start.34
  7.3 305.0 %all-gather.2.cloned.1.call-start = ((), (), s32[]{:S(2)}) async-start(), calls=%async_computation.2 | async-start | bytes 17301504 | tf_op jit(solution)/shard_map/all_gather | solution.py:1156
  13.8 6.8 copy-start.9
  21.3 102.3 %copy-start.28 = (bf16[1,512,1408]{2,1,0:T(8,128)(2,1)S(1)}, bf16[1,512,1408]{2,1,0:T(8,128)(2,1)}, u32[]{:S(2)}) copy-start(bf16[1,512,1408]{2,1,0:T(8,128)(2,1)} %param.36) | copy-start | bytes 4325380
  128.2 5.0 copy-start.2
  128.2 157.0 %all-to-all-start = ((bf16[4,704,512]{2,1,0:T(8,128)(2,1)}), bf16[4,704,512]{2,1,0:T(8,128)(2,1)}, u32[]{:S(2)}, u32[]{:S(2)}) async-start(bf16[4,704,512]{2,1,0:T(8,128)(2,1)} %bitcast.219), calls=%async_computation | async-start | bytes 5767168 | tf_op jit(solution)/shard_map/all_to_all | solution.py:1147
  135.5 3.5 copy-start
  144.5 2.0 copy-start.29
  153.6 5.4 copy-start.13
  154.3 2.3 copy-start.18
  154.3 2.3 copy-start.20
  154.4 2.3 copy-start.22
  154.4 2.3 copy-start.24
  156.7 3.2 copy-start.6
  160.0 5.1 copy-start.33
  165.1 3.3 copy-start.30
  168.4 110.0 %copy-start.5 = (bf16[1,128,2048]{2,1,0:T(8,128)(2,1)S(1)}, bf16[1,128,2048]{2,1,0:T(8,128)(2,1)}, u32[]{:S(2)}) copy-start(bf16[1,128,2048]{2,1,0:T(8,128)(2,1)} %param.21) | copy-start | bytes 1572868
  275.9 5.0 copy-start.38
  278.4 3.7 copy-start.1
  280.3 4.9 copy-start.3
  546.8 2.4 copy-start.17
  549.1 4.0 copy-start.10
  585.8 4.3 copy-start.14
  585.8 10.9 %slice-start = ((s8[8388608]{0:T(1024)(128)(4,1)}), s8[4194304]{0:T(1024)(128)(4,1)S(1)}, s32[]{:S(2)}) async-start(s8[8388608]{0:T(1024)(128)(4,1)} %bitcast.226), calls=%async_computation.3 | async-start | bytes 8388608
  590.1 6.7 slice-start.1
  596.7 4.5 copy-start.23
  596.7 4.5 copy-start.25
  610.2 7.8 copy-start.27
  610.2 7.8 copy-start.35
  610.2 8.1 copy-start.4
  618.0 4.8 copy-start.16
  622.8 5.4 copy-start.31
  622.8 5.4 copy-start.47
  804.7 4.0 copy-start.37
  824.3 65.5 %all-to-all-start.1 = ((bf16[4,704,512]{2,1,0:T(8,128)(2,1)}), bf16[4,704,512]{2,1,0:T(8,128)(2,1)}, u32[]{:S(2)}, u32[]{:S(2)}) async-start(bf16[4,704,512]{2,1,0:T(8,128)(2,1)} %bitcast.220), calls=%async_computation.1 | async-start | bytes 5767168 | tf_op jit(solution)/shard_map/all_to_all | solution.py:1248
  857.6 18.1 %copy-start.15 = (f32[128,2048]{1,0:T(8,128)S(1)}, f32[128,2048]{1,0:T(8,128)}, u32[]{:S(2)}) copy-start(f32[128,2048]{1,0:T(8,128)} %get-tuple-element.58) | copy-start | bytes 3145732
  873.3 2.8 copy-start.46
  874.5 3.8 copy-start.11
  874.5 3.8 copy-start.32
  897.9 2.2 copy-start.36
  (7 other events, 10.8 us)
Sparse Core Ops, SparseCore 0:
  123.8 188.4 all-gather.1

commit v2 on v1

--- a/solution.py
+++ b/solution.py
@@ -360,7 +360,7 @@
         pltpu.make_async_copy(three.at[here.c], three_out.at[here.c, here.z], local.at[1]),
         pltpu.make_async_copy(tokens, x_out.at[here.c], local.at[2]),
         pltpu.make_async_copy(output, output_out.at[here.z], local.at[3]),
-        pltpu.make_async_copy(shared.at[here.c], shared_out.at[:, here.c], local.at[4]),
+        pltpu.make_async_copy(shared.at[:, here.z], shared_out.at[here.z], local.at[4]),
     ]
     for copy in mine:
         copy.start()
@@ -372,8 +372,8 @@
     three_line = LineGather(wire, here, lambda z: three_out.at[:, z])
     output_line = LineGather(wire, here, lambda z: output_out.at[z])
     small_plane = PlaneGather(wire, here, lambda c: small_out.at[c]).first()
-    swapped = [
-        wire.push(shared.at[c], shared_out.at[:, here.c], here.plane(c)) for c in others
+    moved = [
+        wire.push(shared.at[:, z], shared_out.at[here.z], here.line(z)) for z in here.on_line()
     ]
     x_plane.second()
     small_plane.second()
@@ -387,7 +387,7 @@
     output_line.third()
     x_plane.finish()
     small_plane.finish()
-    for copy in swapped:
+    for copy in moved:
         copy.wait_recv()
     three_line.finish()
     output_line.finish()
@@ -397,7 +397,7 @@
 def start_transfers(tokens, three, output, small, shared, later):
     rows, width = tokens.shape
     _, owned, wide = three.shape
-    copies = 3 + 7 + 7 + 2 * PLANE_GATHER_COPIES + 2 * LINE_GATHER_COPIES
+    copies = 3 + 7 + 3 + 2 * PLANE_GATHER_COPIES + 2 * LINE_GATHER_COPIES
     return call(
         start_kernel,
         1,
@@ -419,15 +419,10 @@
 def fold_kernel(parts, shared, out, shared_out, *scratch):
     here, wire = Place(), Wire(scratch[0], scratch[1])
     local = scratch[2]
-    greet(
-        [here.plane(c) for c in (here.twin, here.across, here.along)]
-        + [here.line(z) for z in here.on_line()]
-    )
-    kept = pltpu.make_async_copy(shared.at[here.z], shared_out.at[:, here.z], local.at[2])
+    others = [(here.c + step) % PLANE for step in range(1, PLANE)]
+    greet([here.plane(c) for c in others])
+    kept = pltpu.make_async_copy(shared.at[:, here.c], shared_out.at[here.c], local.at[2])
     kept.start()
-    moved = [
-        wire.push(shared.at[z], shared_out.at[:, here.z], here.line(z)) for z in here.on_line()
-    ]
     half = parts.shape[2] // 2
     jobs, loads = [], []
     for i in range(2):
@@ -440,6 +435,7 @@
     for load, job in zip(loads, jobs):
         load.wait()
         job.begin()
+    moved = [wire.push(shared.at[:, c], shared_out.at[here.c], here.plane(c)) for c in others]
     for job in jobs:
         job.first()
     for job in jobs:
@@ -464,7 +460,7 @@
         3,
         [((rows, width), F32), ((PLANE, LINE) + shared.shape[2:], BF16)],
         [parts.reshape(4, 2, rows, width), shared],
-        wires(2 * PLANE_SCATTER_COPIES + 3)
+        wires(2 * PLANE_SCATTER_COPIES + 7)
         + [pltpu.SemaphoreType.DMA((3,))]
         + held_room(rows // 2, width, BF16) * 2,
         out_specs=[VMEM, HBM],
@@ -575,7 +571,7 @@
         _, z, y = where(step)
         at = pl.ds(4 * y, 4)
         return [
-            pltpu.make_async_copy(o_buf, out_parts.at[z, pl.ds(2 * y, 2)], store.at[0]),
+            pltpu.make_async_copy(o_buf, out_parts.at[pl.ds(2 * y, 2), :, z], store.at[0]),
             pltpu.make_async_copy(p_buf, pre_out.at[z, at], store.at[1]),
             pltpu.make_async_copy(h_buf, weighted_out.at[z, at], store.at[2]),
         ]
@@ -732,7 +728,7 @@
             ((LINE, PLANE, rows, width), BF16),
             ((rows, width), F32),
             (few.shape, F32),
-            ((LINE, 4, 2, rows, width), BF16),
+            ((4, 2, LINE, rows, width), BF16),
             ((LINE, PLANE, rows, 2 * units), BF16),
             ((LINE, PLANE, rows, units), BF16),
         ],
@@ -766,12 +762,9 @@
     )
 
 
-def fan_kernel(block, shared, out, shared_out, send, recv, local):
+def fan_kernel(block, after, out, send, recv, local):
     here, wire = Place(), Wire(send, recv)
-    greet(
-        [here.plane(c) for c in (here.twin, here.across, here.along)]
-        + [here.line(z) for z in here.on_line()]
-    )
+    greet([here.plane(c) for c in (here.twin, here.across, here.along)])
     half = block.shape[0] // 2
     mine = pltpu.make_async_copy(block, out.at[here.c], local.at[0])
     mine.start()
@@ -783,49 +776,38 @@
                 wire, here, functools.partial(lambda at, c: out.at[c, at], at), block.at[at]
             ).first()
         )
-    kept = pltpu.make_async_copy(shared.at[:, here.z], shared_out.at[here.z], local.at[1])
-    kept.start()
-    moved = [
-        wire.push(shared.at[:, z], shared_out.at[here.z], here.line(z)) for z in here.on_line()
-    ]
     for job in jobs:
         job.second()
     for job in jobs:
         job.third()
     for job in jobs:
         job.finish()
-    for copy in moved:
-        copy.wait_recv()
-    kept.wait()
     mine.wait()
     wire.close()
 
 
-def fan_plane(block, shared):
-    out, shared = call(
+def fan_plane(block, after):
+    return call(
         fan_kernel,
         5,
-        [((PLANE,) + block.shape, block.dtype), ((LINE, PLANE) + shared.shape[2:], BF16)],
-        [block, shared],
-        wires(2 * PLANE_GATHER_COPIES + 3) + [pltpu.SemaphoreType.DMA((2,))],
+        [((PLANE,) + block.shape, block.dtype)],
+        [block, after],
+        wires(2 * PLANE_GATHER_COPIES) + [pltpu.SemaphoreType.DMA((1,))],
         in_specs=[VMEM, HBM],
-    )
-    return out.reshape(PLANE * block.shape[0], block.shape[1]), shared
+    )[0].reshape(PLANE * block.shape[0], block.shape[1])
 
 
 def end_kernel(
-    parts, ffn, three, output, shared, bias, terms,
-    out, ffn_out, three_out, output_out, shared_out, bias_out, terms_out,
-    send, recv, local, held, ffn_held, three_held, output_held, *rooms
+    parts, three, output, shared, bias, terms,
+    out, three_out, output_out, shared_mid, shared_out, bias_out, terms_out,
+    send, recv, local, held, three_held, output_held, *rooms
 ):
     here, wire = Place(), Wire(send, recv)
-    room, ffn_rooms = rooms[:5], [rooms[5 + 5 * i : 10 + 5 * i] for i in range(4)]
-    ffn_room, three_room, output_room = rooms[25:27], rooms[27:29], rooms[29:31]
-    terms_in, terms_own, terms_line = rooms[31:]
+    room, three_room, output_room = rooms[:5], rooms[5:7], rooms[7:9]
+    terms_in, terms_own, terms_line = rooms[9:]
     others = [(here.c + step) % PLANE for step in range(1, PLANE)]
     greet([here.plane(c) for c in others] + [here.line(z) for z in here.on_line()])
     on_line = here.on_line()
-    places = [here.mirrored(i) for i in (2, 3, 1, 0)]
     loads = [
         pltpu.make_async_copy(three.at[:, z], three_held.at[z], local.at[z]) for z in range(LINE)
     ]
@@ -835,46 +817,35 @@
         pltpu.make_async_copy(terms.at[here.c], terms_own, local.at[6]),
         pltpu.make_async_copy(bias, bias_out.at[here.z], local.at[7]),
     ]
-    shared_own = pltpu.make_async_copy(shared.at[:, here.c], shared_out.at[here.c], local.at[8])
-    shared_own.start()
-    loads += [
-        pltpu.make_async_copy(ffn.at[z], ffn_held.at[i], local.at[9 + i])
-        for i, z in enumerate(places)
-    ]
-    for copy in loads:
+    shared_own = pltpu.make_async_copy(shared.at[:, here.z], shared_mid.at[here.z], local.at[8])
+    for copy in loads + [shared_own]:
         copy.start()
     job = PlaneScatter(wire, here, held, room)
-    ffn_jobs = [PlaneScatter(wire, here, ffn_held.at[i], ffn_rooms[i]) for i in range(4)]
     three_line = LineScatter(
         wire, here, [three_held.at[here.mirrored(i)] for i in range(4)], three_room
     )
     output_line = LineScatter(
         wire, here, [output_held.at[here.mirrored(i)] for i in range(4)], output_room
     )
-    ffn_line = LineScatter(wire, here, [ffn_jobs[i].mine() for i in (3, 2, 0, 1)], ffn_room)
     for copy in loads[:4]:
         copy.wait()
     three_line.begin()
     loads[4].wait()
     job.begin()
+    shared_line = [
+        wire.push(shared.at[:, z], shared_mid.at[here.z], here.line(z)) for z in on_line
+    ]
     for copy in loads[5:]:
         copy.wait()
+    output_line.begin()
     terms_plane = [
         wire.push(terms.at[c], terms_in.at[j], here.plane(c)) for j, c in enumerate(others)
     ]
-    shared_plane = [
-        wire.push(shared.at[:, c], shared_out.at[here.c], here.plane(c)) for c in others
-    ]
     bias_line = [wire.push(bias, bias_out.at[here.z], here.line(z)) for z in on_line]
-    ffn_jobs[0].begin()
-    ffn_jobs[1].begin()
     job.first()
-    output_line.begin()
-    ffn_jobs[0].first()
     job.second()
-    ffn_jobs[2].begin()
-    ffn_jobs[1].first()
-    ffn_jobs[0].second()
+    job.third()
+    out[...] = job.mine()[...].astype(F32)
     for copy in terms_plane:
         copy.wait_recv()
     total = terms_own[...]
@@ -885,41 +856,32 @@
         wire.push(terms_own.at[z], terms_line.at[j], here.line(z)) for j, z in enumerate(on_line)
     ]
     three_line.first()
-    job.third()
-    out[...] = job.mine()[...].astype(F32)
-    ffn_jobs[3].begin()
-    ffn_jobs[2].first()
-    ffn_jobs[1].second()
-    ffn_jobs[0].third()
-    ffn_jobs[3].first()
-    ffn_jobs[2].second()
-    ffn_jobs[1].third()
+    output_line.first()
     three_line.second()
-    ffn_jobs[3].second()
-    ffn_jobs[2].third()
-    ffn_line.begin()
-    output_line.first()
-    ffn_jobs[3].third()
+    shared_own.wait()
+    for copy in shared_line:
+        copy.wait_recv()
+    shared_kept = pltpu.make_async_copy(shared_mid.at[:, here.c], shared_out.at[here.c], local.at[8])
+    shared_kept.start()
+    shared_plane = [
+        wire.push(shared_mid.at[:, c], shared_out.at[here.c], here.plane(c)) for c in others
+    ]
+    output_line.second()
     three_line.third()
     three_plane = [
         wire.push(three_held.at[here.z, c], three_out.at[here.c], here.plane(c)) for c in others
     ]
     kept = pltpu.make_async_copy(three_held.at[here.z, here.c], three_out.at[here.c], local.at[0])
     kept.start()
-    ffn_line.first()
-    output_line.second()
-    ffn_line.second()
     output_line.third()
     output_out[...] = output_held[here.z].astype(F32)
     for copy in terms_last:
         copy.wait_recv()
     terms_out[...] = terms_own[here.z] + terms_line[0] + terms_line[1] + terms_line[2]
-    ffn_line.third()
-    ffn_out[...] = ffn_held[3 - here.depth, here.y * 2 + here.x, here.core].astype(F32)
     for copy in bias_line + shared_plane + three_plane:
         copy.wait_recv()
     kept.wait()
-    shared_own.wait()
+    shared_kept.wait()
     wire.close()
 
 
@@ -927,33 +889,31 @@
     return [pltpu.VMEM((3,) + shape, kind), pltpu.VMEM((2,) + shape, kind)]
 
 
-def end_transfers(parts, ffn, three, output, shared, bias, terms):
+def end_transfers(parts, three, output, shared, bias, terms):
     rows, width = parts.shape[0] // PLANE, parts.shape[1]
     _, _, owned, wide = three.shape
-    copies = 5 * PLANE_SCATTER_COPIES + 3 * LINE_SCATTER_COPIES + 3 + 7 + 3 + 7 + 7
-    return call(
+    copies = PLANE_SCATTER_COPIES + 2 * LINE_SCATTER_COPIES + 3 + 7 + 3 + 3 + 7 + 7
+    out = call(
         end_kernel,
         6,
         [
             ((rows, width), F32),
-            ((rows, width), F32),
             ((PLANE, owned, wide), BF16),
             ((owned, width), F32),
+            ((LINE, PLANE) + shared.shape[2:], BF16),
             ((PLANE, LINE) + shared.shape[2:], BF16),
             ((LINE,) + bias.shape, F32),
             (terms.shape[2:], F32),
         ],
-        [parts.reshape(4, 2, rows, width), ffn, three, output, shared, bias, terms],
+        [parts.reshape(4, 2, rows, width), three, output, shared, bias, terms],
         wires(copies)
         + [
-            pltpu.SemaphoreType.DMA((13,)),
+            pltpu.SemaphoreType.DMA((9,)),
             pltpu.VMEM((4, 2, rows, width), BF16),
-            pltpu.VMEM((LINE, 4, 2, rows, width), BF16),
             pltpu.VMEM((LINE, PLANE, owned, wide), BF16),
             pltpu.VMEM((LINE, owned, width), BF16),
         ]
-        + scatter_room(rows, width, BF16) * 5
-        + line_room((rows, width), BF16)
+        + scatter_room(rows, width, BF16)
         + line_room((PLANE, owned, wide), BF16)
         + line_room((owned, width), BF16)
         + [
@@ -961,9 +921,10 @@
             pltpu.VMEM(terms.shape[1:], F32),
             pltpu.VMEM((3,) + terms.shape[2:], F32),
         ],
-        out_specs=[VMEM, VMEM, HBM, VMEM, HBM, HBM, VMEM],
-        in_specs=[HBM] * 5 + [VMEM, HBM],
-    )
+        out_specs=[VMEM, HBM, VMEM, HBM, HBM, HBM, VMEM],
+        in_specs=[HBM] * 4 + [VMEM, HBM],
+    )
+    return out[:3] + out[4:]
 
 
 def rms_scale(values):
@@ -1239,12 +1200,15 @@
         x_all, grad_ffn, dots, out_part, grad_pre, weighted = feed_forward(
             normed2, few, g_all, routed, shared, expert_down[0], shared_down, units
         )
+        ffn = scatter_plane(out_part.reshape(plane * line * rows, width))
+        ffn = scatter_line(ffn.reshape(line, rows, width)).astype(F32)
         term_both = outer_sum(
             grad_pre.reshape(line * length, 2 * units), x_all.reshape(line * length, width)
         )
         term_down = outer_sum(weighted.reshape(line * length, units), g_all)
         routed, shared = parts_of(term_both.astype(BF16))
         routed = routed.reshape(2 * routed_units, line, -1).transpose(1, 0, 2)
+        routed_sent = routed
         routed = lax.all_to_all(routed, "fsdp", split_axis=0, concat_axis=0, tiled=True)
         routed = routed.reshape(line, 2, routed_units, -1)
         shared = shared.reshape(2 * shared_units, width).T
@@ -1318,7 +1282,7 @@
 
     grad_branch = grad_mid.astype(BF16)
     if fast:
-        grad_branch, shared = fan_plane(grad_branch, shared)
+        grad_branch = fan_plane(grad_branch, routed_sent)
     else:
         grad_branch = gather_plane(grad_branch)
     routed = routed.transpose(1, 3, 0, 2).reshape(2, 1, -1, line * routed_units).astype(F32)
@@ -1346,9 +1310,8 @@
         count = terms.shape[1]
         terms = terms.reshape(plane, line, owned * count)
         terms = jnp.pad(terms, ((0, 0), (0, 0), (0, 8 * LANES - owned * count)))
-        grad_normed, ffn, grad_three, grad_output, shared, term_bias, terms = end_transfers(
+        grad_normed, grad_three, grad_output, shared, term_bias, terms = end_transfers(
             grad_part,
-            out_part,
             term_three.astype(BF16).reshape(plane, line, owned, 3 * span),
             term_output.astype(BF16).reshape(line, owned, width),
             shared,

time: 916 us -> 878 us (0.959)
  Pallas kernels: 606 us -> 537 us
  waiting for transfers between devices: 36.9 us -> 63.6 us
    pallas_call x5, Pallas kernels: 606 us -> 537 us  [call(): pl.pallas_call(kernel, out_shape=[jax.ShapeDtypeStruct(shape, kind) for s...]
    all_gather x1, waiting for transfers between devices: 27.1 us -> 54.5 us  [body(): g_all = lax.all_gather(g_sent, ('fsdp', 'ctx'), axis=0, tiled=True)]
    all_to_all x2, waiting for transfers between devices: 9.8 us -> 0.01 us  [body(): lax.all_to_all(routed, 'fsdp', split_axis=0, concat_axis=0, tiled=True)]
    unnamed x124 -> x110, local copies, waits for them, and re-layouts: 26.3 us -> 27.6 us
  transfers between devices with their start and end apart: 3 -> 5, of which waited for: 2 -> 2; matrix products, arithmetic and copies ran while one was open for 11% -> 25% of each run, Pallas kernels for 12% -> 25%
where the time goes in v2:
time: 878 us; the launch traced here: 870 us
  Pallas kernels  537 us (61%)
  local copies, waits for them, and re-layouts  111 us (13%)
  matrix products  95.2 us (11%)
  waiting for transfers between devices  63.6 us (7%)
  other arithmetic  38.9 us (4%)
  between operations  14.9 us (2%)
  starting transfers between devices  9.79 us (1%)
    pallas_call x5, Pallas kernels, call(): pl.pallas_call(kernel, out_shape=[jax.ShapeDtypeStruct(shape, kind) for s...  537 us
    all_gather x1, waiting for transfers between devices, body(): g_all = lax.all_gather(g_sent, ('fsdp', 'ctx'), axis=0, tiled=True)  54.5 us
    dot_general x5, matrix products, outer_sum(): lax.dot_general(left, right, (((0,), (0,)), ((), ())), preferred_element_...  53.4 us
    unnamed x110, local copies, waits for them, and re-layouts  27.6 us
  transfers between devices with their start and end apart: 5, of which 2 were waited for; matrix products, arithmetic and copies ran while one was open for 25% of the time, Pallas kernels for 25%

profile of v2, /device:TPU:0, one launch (start us, length us, event | category | flops | bytes accessed | tf_op | source)
XLA Modules:
  0.0 870.0 jit_solution(18363135250944029021)
XLA Ops:
  16.2 2.0 reshape.452
  18.8 3.0 reshape.453
  25.6 113.3 %shard_map.348 = (bf16[8,128,2048]{2,1,0:T(8,128)(2,1)}, bf16[8,4,64,768]{3,2,1,0:T(8,128)(2,1)}, bf16[4,64,2048]{2,1,0:T(8,128)(2,1)}, bf16[8,4,64,128]{3,2,1,0...) custom-call(bf16[128,2048]{1,0:T(8,128)(2,1)} %bitcast.232, ...), custom_call_target="tpu_custom_call", output_to_operand_aliasing={{5}: (5, {})} | custom-call | tf_op jit(solution)/shard_map/pallas_call | solution.py:332
  143.6 4.7 all-to-all-start
  150.6 3.2 multiply_reduce_fusion
  156.0 3.6 convolution_add_fusion.1
  165.4 3.4 fusion.37
  170.1 2.3 select_reduce_fusion
  172.5 2.0 fusion.2
  175.7 5.1 fusion.62
  180.9 3.4 convolution_convert_fusion
  184.2 58.2 %shard_map.349 = (f32[128,2048]{1,0:T(8,128)}, bf16[8,4,64,352]{3,2,1,0:T(8,128)(2,1)}) custom-call(bf16[4,2,128,2048]{3,2,1,0:T(8,128)(2,1)} %bitcast.221, bf16[4,8,64,352]{3,2,1,0:T(8,128)(2,1)} %get-tuple-element.43.shared), custom_call_target="tpu_custom_call" | custom-call | tf_op jit(solution)/shard_map/pallas_call | solution.py:332
  242.5 2.5 copy.228
  248.6 54.5 %all-gather.2.cloned.1.call-done = bf16[4096,2048]{1,0:T(8,128)(2,1)} async-done(((bf16[128,2048]{1,0:T(8,128)(2,1)}), bf16[4096,2048]{1,0:T(8,128)(2,1)}) %all-gather.2.cloned.1.call-update) | async-done | bytes 16777232 | tf_op jit(solution)/shard_map/all_gather | solution.py:1117
  303.1 202.9 %shard_map.350 = (bf16[4,8,128,2048]{3,2,1,0:T(8,128)(2,1)}, f32[128,2048]{1,0:T(8,128)}, f32[16,128]{1,0:T(8,128)}, bf16[4,2,4,128,2048]{4,3,2,1,0:T(8,128)(2,1...) custom-call(bf16[128,2048]{1,0:T(8,128)(2,1)} %copy-done.2, f32[16,128]{1,0:T(8,128)} %pad.13.few, ...), custom_call_target="tpu_custom_call" | custom-call | tf_op jit(solution)/shard_map/pallas_call | solution.py:332
  506.1 5.4 fusion.1
  514.1 2.0 reshape.478
  516.9 30.6 %bitcast_convert_fusion = bf16[1280,2048]{1,0:T(8,128)(2,1)S(1)} fusion(bf16[4,8,128,1280]{3,2,1,0:T(8,128)(2,1)} %get-tuple-element.50, bf16[4,8,128,2048]{3,2,1,0:T(8,128)(2,1)} %get-tuple-element.51), kind=kOutput, calls=%fused_computation | convolution fusion | flops 21477457920 | bytes 32505856 | tf_op jit(solution)/shard_map/dot_general | solution.py:959
  547.5 2.4 copy-done.19
  552.1 7.2 reshape.468
  559.3 4.0 copy.286
  563.2 4.7 all-to-all-start.1
  569.1 37.2 %shard_map.351 = bf16[8,128,2048]{2,1,0:T(8,128)(2,1)} custom-call(bf16[128,2048]{1,0:T(8,128)(2,1)} %fusion.57.block, bf16[4,704,512]{2,1,0:T(8,128)(2,1)} %bitcast.223), custom_call_target="tpu_custom_call" | custom-call | tf_op jit(solution)/shard_map/pallas_call | solution.py:332
  606.4 4.9 multiply_reduce_fusion.4
  611.3 6.1 multiply_convert_fusion
  617.4 2.0 fusion.12
  624.4 2.0 copy.241
  629.1 2.6 copy.243
  631.6 6.3 fusion.13
  638.3 2.2 convolution_convert_fusion.3
  640.5 5.1 convolution_convert_fusion.1
  645.6 4.9 convolution_convert_fusion.2
  651.1 125.2 %shard_map.352 = (f32[128,2048]{1,0:T(8,128)}, bf16[8,64,768]{2,1,0:T(8,128)(2,1)}, f32[64,2048]{1,0:T(8,128)}, bf16[4,8,64,352]{3,2,1,0:T(8,128)(2,1)}, bf16[8,...) custom-call(bf16[4,2,128,2048]{3,2,1,0:T(8,128)(2,1)} %bitcast.243, ...), custom_call_target="tpu_custom_call" | custom-call | tf_op jit(solution)/shard_map/pallas_call | solution.py:332
  776.3 6.4 reshape.493
  782.6 3.5 reshape.491
  786.2 9.3 %fusion.59 = (f32[1,64,32,176]{3,0,1,2:T(1,128)}, f32[1,64,32,176]{3,0,1,2:T(1,128)S(1)}) fusion(f32[2,64,32,176]{3,0,1,2:T(2,128)} %bitcast.226), kind=kLoop, calls=%fused_computation.158 | loop fusion | bytes 5767168 | tf_op jit(solution)/shard_map/slice | solution.py:1328
  795.5 2.1 multiply_reduce_fusion.1
  797.6 2.5 copy.247
  800.1 3.3 squeeze.91
  803.4 4.1 copy.248
  807.5 3.5 squeeze.92
  817.3 15.5 %fusion.65 = f32[640,2048]{1,0:T(8,128)S(1)} fusion(bf16[4096,640]{1,0:T(8,128)(2,1)} %bitcast.302, bf16[4096,2048]{1,0:T(8,128)(2,1)} %all-gather.2.cloned.1.call-done), kind=kOutput, calls=%fused_computation.164 | convolution fusion | flops 10737418240 | bytes 27262976 | tf_op jit(solution)/shard_map/dot_general | solution.py:959
  837.8 2.6 copy_bitcast_fusion
  840.4 3.2 fusion.58
  843.6 3.4 copy.250
  846.9 3.4 copy.251
  850.4 9.0 %reduce-scatter.5.cloned.1.call-done = bf16[1,128,2048]{2,1,0:T(8,128)(2,1)} async-done(((bf16[4,128,2048]{2,1,0:T(8,128)(2,1)}), bf16[1,128,2048]{2,1,0:T(8,128)(2,1)}) %reduce-scatter.5.cloned.1.call-update) | async-done | bytes 524304 | tf_op jit(solution)/shard_map/reduce_scatter | solution.py:971
  859.4 3.0 fusion.26
  (195 shorter events, 61.2 us)
Async XLA Ops:
  7.2 9.0 %copy-start.36 = (bf16[64,5632]{1,0:T(8,128)(2,1)S(1)}, bf16[64,5632]{1,0:T(8,128)(2,1)}, u32[]{:S(2)}) copy-start(bf16[64,5632]{1,0:T(8,128)(2,1)} %param.38) | copy-start | bytes 2162692
  7.2 295.9 %all-gather.2.cloned.1.call-start = ((), (), s32[]{:S(2)}) async-start(), calls=%async_computation.4 | async-start | bytes 17301504 | tf_op jit(solution)/shard_map/all_gather | solution.py:1117
  16.1 6.3 copy-start.9
  23.2 115.8 %copy-start.30 = (bf16[1,512,1408]{2,1,0:T(8,128)(2,1)S(1)}, bf16[1,512,1408]{2,1,0:T(8,128)(2,1)}, u32[]{:S(2)}) copy-start(bf16[1,512,1408]{2,1,0:T(8,128)(2,1)} %param.35) | copy-start | bytes 4325380
  143.6 5.0 copy-start.1
  143.6 105.0 %all-to-all-start = ((bf16[4,704,512]{2,1,0:T(8,128)(2,1)}), bf16[4,704,512]{2,1,0:T(8,128)(2,1)}, u32[]{:S(2)}, u32[]{:S(2)}) async-start(bf16[4,704,512]{2,1,0:T(8,128)(2,1)} %bitcast.227), calls=%async_computation | async-start | bytes 5767168 | tf_op jit(solution)/shard_map/all_to_all | solution.py:1108
  148.4 668.9 %reduce-scatter.3.cloned.1.call-start = ((), (), s32[]{:S(2)}) async-start(), calls=%async_computation.5 | async-start | bytes 18874368 | tf_op jit(solution)/shard_map/reduce_scatter | solution.py:967
  150.6 3.5 copy-start
  154.1 1.9 copy-start.42
  159.5 2.0 copy-start.31
  169.3 5.2 copy-start.14
  170.1 2.3 copy-start.20
  170.1 2.3 copy-start.22
  170.1 2.3 copy-start.24
  170.1 2.3 copy-start.26
  172.5 3.2 copy-start.5
  175.7 5.1 copy-start.35
  180.8 3.4 copy-start.32
  184.2 60.8 %copy-start.4 = (bf16[1,128,2048]{2,1,0:T(8,128)(2,1)S(1)}, bf16[1,128,2048]{2,1,0:T(8,128)(2,1)}, u32[]{:S(2)}) copy-start(bf16[1,128,2048]{2,1,0:T(8,128)(2,1)} %param.21) | copy-start | bytes 1572868
  242.5 4.9 copy-start.40
  246.7 56.4 %copy-start.2 = (bf16[128,2048]{1,0:T(8,128)(2,1)}, bf16[128,2048]{1,0:T(8,128)(2,1)S(1)}, u32[]{:S(2)}) copy-start(bf16[128,2048]{1,0:T(8,128)(2,1)S(1)} %multiply_convert_fusion.2.x) | copy-start | bytes 1572868
  506.1 5.4 copy-start.38
  506.1 5.7 copy-start.3
  506.1 5.9 copy-start.34
  547.5 2.4 copy-start.19
  563.2 4.8 copy-start.10
  563.2 274.6 %all-to-all-start.1 = ((bf16[4,704,512]{2,1,0:T(8,128)(2,1)}), bf16[4,704,512]{2,1,0:T(8,128)(2,1)}, u32[]{:S(2)}, u32[]{:S(2)}) async-start(bf16[4,704,512]{2,1,0:T(8,128)(2,1)} %bitcast.222), calls=%async_computation.3 | async-start | bytes 5767168 | tf_op jit(solution)/shard_map/all_to_all | solution.py:1212
  567.9 291.5 %reduce-scatter.5.cloned.1.call-start = ((), (), s32[]{:S(2)}) async-start(), calls=%async_computation.6 | async-start | bytes 2621440 | tf_op jit(solution)/shard_map/reduce_scatter | solution.py:971
  606.3 4.9 copy-start.15
  611.2 6.1 copy-start.44
  611.2 6.1 copy-start.25
  611.3 6.1 copy-start.27
  617.4 2.0 copy-start.21
  617.4 2.0 copy-start.23
  619.4 1.4 copy-start.8
  619.4 1.4 copy-start.28
  631.6 6.3 copy-start.29
  631.6 6.6 copy-start.17
  631.6 6.6 copy-start.33
  638.0 2.6 copy-start.43
  640.5 5.1 copy-start.16
  786.2 9.3 %copy-start.6 = (f32[8,64,3,256]{3,2,1,0:T(4,128)S(1)}, f32[8,64,3,256]{3,2,1,0:T(4,128)}, u32[]{:S(2)}) copy-start(f32[8,64,3,256]{3,2,1,0:T(4,128)} %reshape.491) | copy-start | bytes 4718596
  786.2 9.3 %copy-start.13 = (bf16[3,64,8,256]{3,2,1,0:T(8,128)(2,1)S(1)}, bf16[3,64,8,256]{3,2,1,0:T(8,128)(2,1)}, u32[]{:S(2)}) copy-start(bf16[3,64,8,256]{3,2,1,0:T(8,128)(2,1)} %copy-done.12) | copy-start | bytes 2359300
  807.5 7.8 copy-start.39
  817.2 17.9 %copy-start.18 = (f32[128,2048]{1,0:T(8,128)S(1)}, f32[128,2048]{1,0:T(8,128)}, u32[]{:S(2)}) copy-start(f32[128,2048]{1,0:T(8,128)} %get-tuple-element.52) | copy-start | bytes 3145732
  832.7 2.8 copy-start.41
  846.9 12.5 %copy-start.11 = (bf16[1,128,2048]{2,1,0:T(8,128)(2,1)S(1)}, bf16[1,128,2048]{2,1,0:T(8,128)(2,1)}, u32[]{:S(2)}) copy-start(bf16[1,128,2048]{2,1,0:T(8,128)(2,1)} %param.24) | copy-start | bytes 1572868
  859.4 3.0 copy-start.37
  (2 other events, 2.2 us)
Sparse Core Ops, SparseCore 0:
  139.1 163.9 all-gather.1
  506.1 128.2 reduce-scatter.2
  817.4 41.9 reduce-scatter.4

commit v3 on v2

--- a/solution.py
+++ b/solution.py
@@ -343,8 +343,8 @@
 
 
 def start_kernel(
-    tokens, three, output, small, shared, later, x_out, three_out, output_out, small_out,
-    shared_out, later_out, send, recv, local
+    tokens, three, output, small, shared, x_out, three_out, output_out, small_out, shared_out,
+    send, recv, local
 ):
     here, wire = Place(), Wire(send, recv)
     others = [(here.c + step) % PLANE for step in range(1, PLANE)]
@@ -394,7 +394,7 @@
     wire.close()
 
 
-def start_transfers(tokens, three, output, small, shared, later):
+def start_transfers(tokens, three, output, small, shared):
     rows, width = tokens.shape
     _, owned, wide = three.shape
     copies = 3 + 7 + 3 + 2 * PLANE_GATHER_COPIES + 2 * LINE_GATHER_COPIES
@@ -407,12 +407,10 @@
             ((LINE, owned, width), BF16),
             ((PLANE, LINE) + small.shape, BF16),
             ((LINE, PLANE) + shared.shape[2:], BF16),
-            (later.shape, later.dtype),
         ],
-        [tokens, three, output, small, shared, later],
+        [tokens, three, output, small, shared],
         wires(copies) + [pltpu.SemaphoreType.DMA((5,))],
-        in_specs=[VMEM] * 5 + [HBM],
-        aliases={5: 5},
+        in_specs=[VMEM] * 5,
     )
 
 
@@ -1096,13 +1094,13 @@
         marks = small.shape[1]
         small = jnp.pad(small, ((0, 0), (0, LANES - marks)))
         sent = three.reshape(3, owned, plane, span).transpose(2, 1, 0, 3)
-        x_all, w_three, w_output, small, shared, g_sent = start_transfers(
+        g_all = lax.all_gather(g_own, ("fsdp", "ctx"), axis=0, tiled=True)
+        x_all, w_three, w_output, small, shared = start_transfers(
             x_own,
             sent.reshape(plane, owned, 3 * span),
             output_weight,
             small,
             shared.reshape(plane, line, owned, 2 * shared_units),
-            g_own,
         )
         routed = routed.reshape(line, 2 * routed_units, -1)
         routed = lax.all_to_all(routed, "fsdp", split_axis=0, concat_axis=0, tiled=True)
@@ -1114,7 +1112,6 @@
         digits = digits.transpose(0, 2, 1).reshape(plane, 2, rows)
         places = (digits[:, 0] * 64 + digits[:, 1]).reshape(length)
         small = small.reshape(width, LANES)[:, : columns.shape[1]]
-        g_all = lax.all_gather(g_sent, ("fsdp", "ctx"), axis=0, tiled=True)
     else:
         small = lax.all_gather(columns, BOTH, axis=0, tiled=True)
         places = lax.all_gather(positions[0], "ctx", axis=0, tiled=True)
@@ -1323,9 +1320,11 @@
         term_bias = jnp.sum(term_bias[:, 0], axis=0).reshape(3, line, owned)
         grad_bias = lax.dynamic_index_in_dim(term_bias, lax.axis_index("fsdp"), 1, keepdims=False)
         terms = terms.reshape(-1)[: owned * count].reshape(owned, count)
-        shared = shared.reshape(plane * line, owned, 2, shared_units).transpose(2, 1, 0, 3)
-        shared = shared.reshape(2, owned, -1).astype(F32)
-        grad_shared_gate, grad_shared_up = shared[0], shared[1]
+        shared = shared.reshape(plane * line, owned, 2 * shared_units)
+        grad_shared_gate, grad_shared_up = [
+            part.transpose(1, 0, 2).reshape(owned, -1).astype(F32)
+            for part in (shared[:, :, :shared_units], shared[:, :, shared_units:])
+        ]
     else:
         grad_normed = scatter_plane(grad_part).astype(F32)
         zeros = jnp.zeros((3, width, width), BF16)

time: 878 us -> 914 us (1.041)
  Pallas kernels: 537 us -> 637 us
  waiting for transfers between devices: 63.6 us -> 11 us
  local copies, waits for them, and re-layouts: 111 us -> 94 us
    pallas_call x5, Pallas kernels: 537 us -> 637 us  [call(): pl.pallas_call(kernel, out_shape=[jax.ShapeDtypeStruct(shape, kind) for s...]
    all_gather x1, waiting for transfers between devices: 54.5 us -> 0.01 us  [body(): g_all = lax.all_gather(g_own, ('fsdp', 'ctx'), axis=0, tiled=True)]
    slice x3 -> x0, local copies, waits for them, and re-layouts: 15.9 us -> none  [body(): grad_shared_gate, grad_shared_up = (shared[0], shared[1])]
    unnamed x110 -> x125, local copies, waits for them, and re-layouts: 27.6 us -> 25.1 us
  transfers between devices with their start and end apart: 5 -> 5, of which waited for: 2 -> 1; matrix products, arithmetic and copies ran while one was open for 25% -> 25% of each run, Pallas kernels for 25% -> 48%
where the time goes in v3:
time: 914 us; the launch traced here: 907 us
  Pallas kernels  637 us (70%)
  matrix products  94.5 us (10%)
  local copies, waits for them, and re-layouts  94 us (10%)
  other arithmetic  44.6 us (5%)
  between operations  15 us (2%)
  starting transfers between devices  11.2 us (1%)
  waiting for transfers between devices  11 us (1%)
    pallas_call x5, Pallas kernels, call(): pl.pallas_call(kernel, out_shape=[jax.ShapeDtypeStruct(shape, kind) for s...  637 us
    dot_general x5, matrix products, outer_sum(): lax.dot_general(left, right, (((0,), (0,)), ((), ())), preferred_element_...  53.4 us
    unnamed x125, local copies, waits for them, and re-layouts  25.1 us
  transfers between devices with their start and end apart: 5, of which 1 were waited for; matrix products, arithmetic and copies ran while one was open for 25% of the time, Pallas kernels for 48%

profile of v3, /device:TPU:0, one launch (start us, length us, event | category | flops | bytes accessed | tf_op | source)
XLA Modules:
  0.0 907.5 jit_solution(5852107617923700246)
XLA Ops:
  9.6 2.5 copy.225
  15.8 6.5 all-to-all-start
  25.4 3.0 reshape.452
  29.0 3.2 reshape.453
  35.3 230.0 %shard_map.348 = (bf16[8,128,2048]{2,1,0:T(8,128)(2,1)}, bf16[8,4,64,768]{3,2,1,0:T(8,128)(2,1)}, bf16[4,64,2048]{2,1,0:T(8,128)(2,1)}, bf16[8,4,64,128]{3,2,1,0:T(8,128)(2,1)}, bf16[4,8,64,352]{3,2,1,0:T(8,128)(2,1)}) custom-call(bf16[128,2048]{1,0:T(8,128)(2,1)} %bitcast.232, bf16[8,64,768]{2,1,0:T(8,128)(2,1)} %reshape.451.three, ...), custom_call_target="tpu_custom_call" | custom-call | tf_op jit(solution)/shard_map/pallas_call | solution.py:332
  266.5 2.8 slice_reduce_fusion
  269.8 3.2 multiply_reduce_fusion
  275.1 3.6 convolution_add_fusion.1
  284.7 3.4 fusion.39
  289.4 2.3 select_reduce_fusion
  291.8 2.0 fusion.4
  295.0 5.1 fusion.63
  300.1 3.3 convolution_convert_fusion
  303.5 41.4 %shard_map.349 = (f32[128,2048]{1,0:T(8,128)}, bf16[8,4,64,352]{3,2,1,0:T(8,128)(2,1)}) custom-call(bf16[4,2,128,2048]{3,2,1,0:T(8,128)(2,1)} %bitcast.222, bf16[4,8,64,352]{3,2,1,0:T(8,128)(2,1)} %get-tuple-element.42.shared), custom_call_target="tpu_custom_call" | custom-call | tf_op jit(solution)/shard_map/pallas_call | solution.py:332
  344.9 2.5 copy.227
  351.0 203.3 %shard_map.350 = (bf16[4,8,128,2048]{3,2,1,0:T(8,128)(2,1)}, f32[128,2048]{1,0:T(8,128)}, f32[16,128]{1,0:T(8,128)}, bf16[4,2,4,128,2048]{4,3,2,1,0:T(8,128)(2,1...) custom-call(bf16[128,2048]{1,0:T(8,128)(2,1)} %copy-done.2, f32[16,128]{1,0:T(8,128)} %pad.13.few, ...), custom_call_target="tpu_custom_call" | custom-call | tf_op jit(solution)/shard_map/pallas_call | solution.py:332
  554.5 5.4 fusion.3
  562.5 2.0 reshape.478
  565.2 30.7 %bitcast_convert_fusion = bf16[1280,2048]{1,0:T(8,128)(2,1)S(1)} fusion(bf16[4,8,128,1280]{3,2,1,0:T(8,128)(2,1)} %get-tuple-element.48, bf16[4,8,128,2048]{3,2,1,0:T(8,128)(2,1)} %get-tuple-element.49), kind=kOutput, calls=%fused_computation.2 | convolution fusion | flops 21477457920 | bytes 32505856 | tf_op jit(solution)/shard_map/dot_general | solution.py:957
  595.9 2.4 copy-done.17
  600.4 7.1 reshape.468
  607.5 4.0 copy.285
  611.5 4.7 all-to-all-start.1
  617.4 37.9 %shard_map.351 = bf16[8,128,2048]{2,1,0:T(8,128)(2,1)} custom-call(bf16[128,2048]{1,0:T(8,128)(2,1)} %fusion.59.block, bf16[4,704,512]{2,1,0:T(8,128)(2,1)} %bitcast.224), custom_call_target="tpu_custom_call" | custom-call | tf_op jit(solution)/shard_map/pallas_call | solution.py:332
  655.4 4.2 multiply_reduce_fusion.4
  659.6 6.1 multiply_convert_fusion
  671.4 2.0 copy.236
  673.5 2.1 copy.240
  678.3 2.6 copy.242
  680.8 6.3 fusion.15
  687.5 2.3 convolution_convert_fusion.3
  689.7 5.0 convolution_convert_fusion.1
  694.8 4.9 convolution_convert_fusion.2
  700.3 124.4 %shard_map.352 = (f32[128,2048]{1,0:T(8,128)}, bf16[8,64,768]{2,1,0:T(8,128)(2,1)}, f32[64,2048]{1,0:T(8,128)}, bf16[4,8,64,352]{3,2,1,0:T(8,128)(2,1)}, bf16[8,...) custom-call(bf16[4,2,128,2048]{3,2,1,0:T(8,128)(2,1)} %bitcast.242, ...), custom_call_target="tpu_custom_call" | custom-call | tf_op jit(solution)/shard_map/pallas_call | solution.py:332
  824.7 3.7 reshape.494
  828.4 3.5 convert_bitcast_fusion
  831.9 2.2 multiply_reduce_fusion.1
  834.1 2.5 copy.246
  836.6 3.3 reshape.491
  839.9 4.1 copy.247
  844.0 3.3 reshape.492
  853.5 15.5 %fusion = f32[640,2048]{1,0:T(8,128)S(1)} fusion(bf16[4096,640]{1,0:T(8,128)(2,1)} %bitcast.302, bf16[1,4096,2048]{2,1,0:T(8,128)(2,1)} %all-gather.3.cloned.1.call-done), kind=kOutput, calls=%fused_computation | convolution fusion | flops 10737418240 | bytes 27262976 | tf_op jit(solution)/shard_map/dot_general | solution.py:957
  874.1 2.6 copy_bitcast_fusion
  876.7 3.2 fusion.60
  879.9 3.4 copy.249
  883.3 3.4 copy.250
  886.6 10.3 %reduce-scatter.5.cloned.1.call-done = bf16[1,128,2048]{2,1,0:T(8,128)(2,1)} async-done(((bf16[4,128,2048]{2,1,0:T(8,128)(2,1)}), bf16[1,128,2048]{2,1,0:T(8,128)(2,1)}) %reduce-scatter.5.cloned.1.call-update) | async-done | bytes 524304 | tf_op jit(solution)/shard_map/reduce_scatter | solution.py:969
  896.9 3.0 fusion.28
  (209 shorter events, 56.2 us)
Async XLA Ops:
  7.2 343.8 %all-gather.3.cloned.1.call-start = ((), (), s32[]{:S(2)}) async-start(), calls=%async_computation.6 | async-start | bytes 17301504 | tf_op jit(solution)/shard_map/all_gather | solution.py:1097
  15.7 6.6 copy-start.51
  15.7 6.7 copy-start.41
  15.7 6.7 copy-start.42
  15.7 6.7 copy-start.43
  15.7 6.7 copy-start.44
  15.7 6.7 copy-start.45
  15.7 6.7 copy-start.46
  15.7 6.7 copy-start.47
  15.7 7.0 copy-start.35
  15.7 7.0 copy-start.36
  15.8 7.1 copy-start.37
  15.8 335.3 %all-to-all-start = ((bf16[4,704,512]{2,1,0:T(8,128)(2,1)}), bf16[4,704,512]{2,1,0:T(8,128)(2,1)}, u32[]{:S(2)}, u32[]{:S(2)}) async-start(bf16[4,704,512]{2,1,0:T(8,128)(2,1)} %bitcast.227), calls=%async_computation | async-start | bytes 5767168 | tf_op jit(solution)/shard_map/all_to_all | solution.py:1106
  22.2 831.3 %reduce-scatter.3.cloned.1.call-start = ((), (), s32[]{:S(2)}) async-start(), calls=%async_computation.4 | async-start | bytes 18874368 | tf_op jit(solution)/shard_map/reduce_scatter | solution.py:965
  23.0 9.3 %copy-start.10 = (bf16[3,64,8,256]{3,2,1,0:T(8,128)(2,1)}, bf16[3,64,8,256]{3,2,1,0:T(8,128)(2,1)S(1)}, u32[]{:S(2)}) copy-start(bf16[3,64,8,256]{3,2,1,0:T(8,128)(2,1)S(1)} %bitcast_dynamic-update-slice_fusion) | copy-start | bytes 2359300
  269.8 3.5 copy-start
  278.7 4.0 copy-start.1
  288.6 5.2 copy-start.12
  289.4 2.3 copy-start.18
  289.4 2.3 copy-start.20
  291.8 3.2 copy-start.4
  295.0 5.1 copy-start.33
  300.1 44.8 %copy-start.30 = (bf16[1024,2,128]{0,2,1:T(8,128)(2,1)}, bf16[1024,2,128]{0,2,1:T(8,128)(2,1)S(1)}, u32[]{:S(2)}) copy-start(bf16[1024,2,128]{0,2,1:T(8,128)(2,1)S(1)} %get-tuple-element.184) | copy-start | bytes 1572868
  303.5 44.0 %copy-start.6 = (bf16[1,128,2048]{2,1,0:T(8,128)(2,1)S(1)}, bf16[1,128,2048]{2,1,0:T(8,128)(2,1)}, u32[]{:S(2)}) copy-start(bf16[1,128,2048]{2,1,0:T(8,128)(2,1)} %param.21) | copy-start | bytes 1572868
  344.9 4.9 copy-start.40
  554.4 5.5 copy-start.38
  554.4 5.7 copy-start.3
  554.4 5.9 copy-start.32
  595.9 2.4 copy-start.17
  611.5 4.8 copy-start.9
  611.5 262.6 %all-to-all-start.1 = ((bf16[4,704,512]{2,1,0:T(8,128)(2,1)}), bf16[4,704,512]{2,1,0:T(8,128)(2,1)}, u32[]{:S(2)}, u32[]{:S(2)}) async-start(bf16[4,704,512]{2,1,0:T(8,128)(2,1)} %bitcast.223), calls=%async_computation.3 | async-start | bytes 5767168 | tf_op jit(solution)/shard_map/all_to_all | solution.py:1209
  616.2 280.7 %reduce-scatter.5.cloned.1.call-start = ((), (), s32[]{:S(2)}) async-start(), calls=%async_computation.5 | async-start | bytes 2621440 | tf_op jit(solution)/shard_map/reduce_scatter | solution.py:969
  655.4 4.2 copy-start.13
  659.5 6.2 copy-start.52
  659.6 6.2 copy-start.23
  659.6 6.2 copy-start.25
  680.8 6.3 copy-start.27
  680.8 6.4 copy-start.28
  680.8 6.7 copy-start.15
  680.8 6.7 copy-start.31
  687.2 2.6 copy-start.50
  689.7 5.0 copy-start.14
  828.4 3.5 copy-start.5
  828.4 3.5 copy-start.11
  844.0 7.6 copy-start.39
  853.5 17.9 %copy-start.16 = (f32[128,2048]{1,0:T(8,128)S(1)}, f32[128,2048]{1,0:T(8,128)}, u32[]{:S(2)}) copy-start(f32[128,2048]{1,0:T(8,128)} %get-tuple-element.50) | copy-start | bytes 3145732
  869.0 2.8 copy-start.48
  896.9 3.0 copy-start.34
  (10 other events, 18.6 us)
Sparse Core Ops, SparseCore 0:
  10.9 201.2 all-gather.2
  554.5 130.5 reduce-scatter.2
  853.7 43.2 reduce-scatter.4
